TPU v7x, 256 devices: a whole 4x4x8 slice. The times are simulated.
256 devices in a mesh: dp: 8 (over x_lo, y), expert: 32 (over z, x_hi, core).
Axes of the slice: x: 4 (x_hi: 2, x_lo: 2; x = x_hi * 2 + x_lo), y: 4, z: 8, core: 2. Of those that a mesh axis runs over, the one named last changes fastest.
Arguments:
- tokens: bfloat16 [65536, 1280], P(('dp', 'expert')), may hold values from -68 to 68
- router: bfloat16 [1280, 128], replicated, may hold values from -0.5 to 0.5
- expert_in: bfloat16 [64, 1280, 3072], P('expert', None, 'dp'), may hold values from -1.25 to 1.25
- expert_out: bfloat16 [64, 3072, 1280], P('expert', 'dp'), may hold values from -0.625 to 0.625
- cotangent: bfloat16 [65536, 1280], P(('dp', 'expert')), may hold values from -6 to 6
Outputs:
- mixed: bfloat16 [65536, 1280], P(('dp', 'expert'))
- grad_tokens: bfloat16 [65536, 1280], P(('dp', 'expert'))
- grad_router: float32 [1280, 128], replicated
- grad_in: bfloat16 [64, 1280, 3072], P('expert', None, 'dp')
- grad_out: bfloat16 [64, 3072, 1280], P('expert', 'dp')
All inputs are finite; a program needn't handle non-finite values.
Results may differ from a plain program's by a relative error of at most 0.023.
Values may be sent and summed in bfloat16 or wider, within the bound.
No kernel may reach another device: no remote copies, remote signals or barrier semaphores. Data moves between devices by JAX's collectives and lax.ppermute only.
A program may use at most 64 MiB of HBM per device.

v0:
```python
import jax
import jax.numpy as jnp
from jax import lax
from jax.sharding import PartitionSpec as P


def gelu_exact(values):
    return jax.nn.gelu(values, approximate=False)


def rounded_terms(form, source, weight):
    terms = jnp.einsum(form, source, weight, preferred_element_type=jnp.float32).astype(
        jnp.bfloat16
    )
    return terms


def to_experts(slot_block):
    moved = lax.all_to_all(slot_block, "expert", split_axis=0, concat_axis=0, tiled=True)
    return lax.all_gather(moved, "dp", axis=0, tiled=True)


def from_experts(source, weight, form):
    held = lax.optimization_barrier(rounded_terms(form, source, weight))
    summed = lax.psum_scatter(
        held.astype(jnp.float32).astype(jnp.bfloat16), "dp", scatter_dimension=0, tiled=True
    )
    return lax.all_to_all(summed, "expert", split_axis=0, concat_axis=0, tiled=True)


def per_device(tokens, router, expert_in, expert_out, cotangent):
    n_expert = lax.axis_size("expert")
    slots_total = router.shape[1]
    local_experts = expert_in.shape[0]
    per_expert = slots_total // (n_expert * local_experts)
    model_width = tokens.shape[1]
    over_tokens = (((0,), (0,)), ((), ()))
    over_width = (((1,), (1,)), ((), ()))
    logits = jnp.dot(tokens, router, preferred_element_type=jnp.float32)
    dispatch = jax.nn.softmax(logits, axis=0)
    combine = jax.nn.softmax(logits, axis=1)
    dispatch_b = dispatch.astype(jnp.bfloat16)
    combine_b = combine.astype(jnp.bfloat16)
    slot_inputs = lax.dot_general(
        dispatch_b, tokens, over_tokens, preferred_element_type=jnp.float32
    ).astype(jnp.bfloat16)
    block_shape = (n_expert, local_experts, per_expert, model_width)
    gathered = to_experts(slot_inputs.reshape(block_shape))
    hidden = jnp.einsum("rjkd,jdf->rjkf", gathered, expert_in, preferred_element_type=jnp.float32)
    activated = gelu_exact(hidden).astype(jnp.bfloat16)
    slot_outputs = from_experts(activated, expert_out, "rjkf,jfd->rjkd").reshape(
        slots_total, model_width
    )
    mixed = jnp.dot(combine_b, slot_outputs, preferred_element_type=jnp.float32).astype(
        jnp.bfloat16
    )
    grad_combine = lax.dot_general(
        cotangent, slot_outputs, over_width, preferred_element_type=jnp.float32
    )
    grad_slot_out = lax.dot_general(
        combine_b, cotangent, over_tokens, preferred_element_type=jnp.float32
    ).astype(jnp.bfloat16)
    logit_combine = combine * (
        grad_combine - jnp.sum(combine * grad_combine, axis=1, keepdims=True)
    )
    grad_gathered = to_experts(grad_slot_out.reshape(block_shape))
    grad_act = jnp.einsum(
        "rjkd,jfd->rjkf", grad_gathered, expert_out, preferred_element_type=jnp.float32
    )
    grad_hidden = jax.vjp(gelu_exact, hidden)[1](grad_act)[0].astype(jnp.bfloat16)
    grad_out = jnp.einsum(
        "rjkf,rjkd->jfd", activated, grad_gathered, preferred_element_type=jnp.float32
    ).astype(jnp.bfloat16)
    grad_in = jnp.einsum(
        "rjkd,rjkf->jdf", gathered, grad_hidden, preferred_element_type=jnp.float32
    ).astype(jnp.bfloat16)
    grad_slot_in = from_experts(grad_hidden, expert_in, "rjkf,jdf->rjkd").reshape(
        slots_total, model_width
    )
    grad_dispatch = lax.dot_general(
        tokens, grad_slot_in, over_width, preferred_element_type=jnp.float32
    )
    logit_dispatch = dispatch * (
        grad_dispatch - jnp.sum(dispatch * grad_dispatch, axis=0, keepdims=True)
    )
    grad_logits = (logit_combine + logit_dispatch).astype(jnp.bfloat16)
    through_slots = jnp.dot(dispatch_b, grad_slot_in, preferred_element_type=jnp.float32)
    through_router = lax.dot_general(
        grad_logits, router, over_width, preferred_element_type=jnp.float32
    )
    grad_tokens = (through_slots + through_router).astype(jnp.bfloat16)
    router_term = lax.dot_general(
        tokens, grad_logits, over_tokens, preferred_element_type=jnp.float32
    )
    grad_router = lax.psum(router_term, ("dp", "expert"))
    return (mixed, grad_tokens, grad_router, grad_in, grad_out)


def solution(mesh):
    in_specs = (
        P(("dp", "expert"), None),
        P(),
        P("expert", None, "dp"),
        P("expert", "dp", None),
        P(("dp", "expert"), None),
    )
    out_specs = (
        P(("dp", "expert"), None),
        P(("dp", "expert"), None),
        P(),
        P("expert", None, "dp"),
        P("expert", "dp", None),
    )
    return jax.shard_map(
        per_device, mesh=mesh, in_specs=in_specs, out_specs=out_specs, check_vma=False
    )
```

profile of v0, /device:TPU:1, one launch (start us, length us, event | category | flops | bytes accessed | tf_op | source)
XLA Modules:
  0.0 518.2 jit_solution(4738159780325384635)
XLA Ops:
  7.2 1.7 fusion.46
  9.1 1.4 convolution_convert_fusion.4
  10.7 25.7 %all_to_all.20 = bf16[32,2,2,1280]{3,2,1,0:T(2,128)(2,1)S(1)} all-to-all(bf16[32,2,2,1280]{3,2,1,0:T(2,128)(2,1)S(1)} %reshape.28), channel_id=1, replica_groups=mesh['dp'=8,'expert'=32] {'expert'}, dimensions={0} | all-to-all | bytes 655360 | tf_op jit(solution)/shard_map/all_to_all | solution.py:19
  36.4 0.8 copy.24
  37.2 0.4 convolution_convert_fusion.3
  37.8 18.3 %all_to_all.21 = bf16[32,2,2,1280]{3,2,1,0:T(2,128)(2,1)S(1)} all-to-all(bf16[32,2,2,1280]{3,2,1,0:T(2,128)(2,1)S(1)} %reshape.30), channel_id=1, replica_groups=mesh['dp'=8,'expert'=32] {'expert'}, dimensions={0} | all-to-all | bytes 655360 | tf_op jit(solution)/shard_map/all_to_all | solution.py:19
  56.0 0.8 copy.26
  56.9 20.5 %all-gather.3.cloned.1.call-done = bf16[256,2,2,1280]{3,0,2,1:T(8,128)(2,1)} async-done(((bf16[32,2,2,1280]{3,0,2,1:T(8,128)(2,1)}), bf16[256,2,2,1280]{3,0,2,1:T(8,128)(2,1)}) %all-gather.3.cloned.1.call-update) | async-done | bytes 2621456 | tf_op jit(solution)/shard_map/all_gather | solution.py:20
  77.4 8.1 %fusion.18 = (bf16[256,2,2,384]{3,0,2,1:T(8,128)(2,1)S(1)}, f32[256,2,2,384]{3,0,2,1:T(8,128)}, f32[2,256,2,384]{3,1,2,0:T(8,128)}) fusion(bf16[256,2,2,1280]{3,0,2,1:T(8,128)(2,1)} %all-gather.3.cloned.1.call-done, bf16[2,1280,384]{2,1,0:T(8,128)(2,1)S(1)} %copy-done), kind=kOutput, calls=%fused_computation.35 | convolution fusion | flops 1032192000 | bytes 8519680 | tf_op jit(solution)/shard_map/rjkd,jdf->rjkf/dot_general | solution.py:49
  85.5 38.7 %all-gather.5.cloned.1.call-done = bf16[256,2,2,1280]{3,0,2,1:T(8,128)(2,1)} async-done(((bf16[32,2,2,1280]{3,0,2,1:T(8,128)(2,1)}), bf16[256,2,2,1280]{3,0,2,1:T(8,128)(2,1)}) %all-gather.5.cloned.1.call-update) | async-done | bytes 2621456 | tf_op jit(solution)/shard_map/all_gather | solution.py:20
  124.2 5.0 fusion.15
  129.2 0.9 copy-done.4
  130.1 3.1 fusion.1
  133.3 4.6 fusion
  137.9 40.9 %reduce-scatter.5.cloned.1.call-done = bf16[32,2,2,1280]{3,0,2,1:T(8,128)(2,1)} async-done(((bf16[256,2,2,1280]{3,0,2,1:T(8,128)(2,1)}), bf16[32,2,2,1280]{3,0,2,1:T(8,128)(2,1)}) %reduce-scatter.5.cloned.1.call-update) | async-done | bytes 327696 | tf_op jit(solution)/shard_map/reduce_scatter | solution.py:25
  178.8 2.0 copy.27
  180.8 14.5 %all-to-all-start.3 = ((bf16[32,2,2,1280]{3,2,1,0:T(2,128)(2,1)}), bf16[32,2,2,1280]{3,2,1,0:T(2,128)(2,1)S(1)}, u32[]{:S(2)}, u32[]{:S(2)}) async-start(bf16[32,2,2,1280]{3,2,1,0:T(2,128)(2,1)} %copy.27), calls=%async_computation.5 | async-start | bytes 655360 | tf_op jit(solution)/shard_map/all_to_all | solution.py:28
  195.3 4.7 bitcast_convert_fusion
  200.0 29.1 %reduce-scatter.3.cloned.1.call-done = bf16[32,2,2,1280]{3,0,2,1:T(8,128)(2,1)} async-done(((bf16[256,2,2,1280]{3,0,2,1:T(8,128)(2,1)}), bf16[32,2,2,1280]{3,0,2,1:T(8,128)(2,1)}) %reduce-scatter.3.cloned.1.call-update) | async-done | bytes 327696 | tf_op jit(solution)/shard_map/reduce_scatter | solution.py:25
  229.1 2.0 copy.25
  231.2 14.6 %all-to-all-start.1 = ((bf16[32,2,2,1280]{3,2,1,0:T(2,128)(2,1)}), bf16[32,2,2,1280]{3,2,1,0:T(2,128)(2,1)}, u32[]{:S(2)}, u32[]{:S(2)}) async-start(bf16[32,2,2,1280]{3,2,1,0:T(2,128)(2,1)} %copy.25), calls=%async_computation.2 | async-start | bytes 655360 | tf_op jit(solution)/shard_map/all_to_all | solution.py:28
  246.0 4.8 bitcast_convert_fusion.1
  251.2 1.4 fusion.37
  252.6 6.5 %all-to-all-done.1 = bf16[32,2,2,1280]{3,2,1,0:T(2,128)(2,1)} async-done(((bf16[32,2,2,1280]{3,2,1,0:T(2,128)(2,1)}), bf16[32,2,2,1280]{3,2,1,0:T(2,128)(2,1)}, u32[]{:S(2)}, u32[]{:S(2)}) %all-to-all-start.1) | async-done | bytes 327712 | tf_op jit(solution)/shard_map/all_to_all | solution.py:28
  259.1 1.1 reshape.29
  260.2 1.6 multiply_reduce_fusion.1
  261.9 0.6 copy-done.7
  262.5 1.3 convolution_bitcast_fusion
  263.8 2.3 convolution_convert_fusion.2
  266.1 2.3 fusion.2
  268.5 241.1 %all-reduce.2.cloned.1.call-done = f32[1280,128]{0,1:T(8,128)} async-done(((f32[1280,128]{0,1:T(8,128)}), f32[1280,128]{0,1:T(8,128)}) %all-reduce.2.cloned.1.call-update) | async-done | bytes 655376 | tf_op jit(solution)/shard_map/psum | solution.py:95
  509.5 2.2 copy.31
  (34 shorter events, 1.4 us)
Async XLA Ops:
  7.2 70.2 %copy-start = (bf16[2,1280,384]{2,1,0:T(8,128)(2,1)S(1)}, bf16[2,1280,384]{2,1,0:T(8,128)(2,1)}, u32[]{:S(2)}) copy-start(bf16[2,1280,384]{2,1,0:T(8,128)(2,1)} %param.7) | copy-start | bytes 5898244
  7.2 70.2 %all-gather.3.cloned.1.call-start = ((), (), s32[]{:S(2)}) async-start(), calls=%async_computation.6 | async-start | bytes 2949120 | tf_op jit(solution)/shard_map/all_gather | solution.py:20
  9.1 28.1 %copy-start.6 = (bf16[256,1280]{1,0:T(8,128)(2,1)S(1)}, bf16[256,1280]{1,0:T(8,128)(2,1)}, u32[]{:S(2)}) copy-start(bf16[256,1280]{1,0:T(8,128)(2,1)} %param.9) | copy-start | bytes 1966084
  37.2 87.0 %all-gather.5.cloned.1.call-start = ((), (), s32[]{:S(2)}) async-start(), calls=%async_computation.8 | async-start | bytes 2949120 | tf_op jit(solution)/shard_map/all_gather | solution.py:20
  56.8 122.0 %reduce-scatter.5.cloned.1.call-start = ((), (), s32[]{:S(2)}) async-start(), calls=%async_computation.9 | async-start | bytes 2949120 | tf_op jit(solution)/shard_map/reduce_scatter | solution.py:25
  85.5 47.8 %copy-start.5 = (bf16[256,2,2,384]{3,0,2,1:T(8,128)(2,1)}, bf16[256,2,2,384]{3,0,2,1:T(8,128)(2,1)S(1)}, u32[]{:S(2)}) copy-start(bf16[256,2,2,384]{3,0,2,1:T(8,128)(2,1)S(1)} %get-tuple-element.26) | copy-start | bytes 2359300
  129.2 0.9 copy-start.4
  133.2 95.9 %reduce-scatter.3.cloned.1.call-start = ((), (), s32[]{:S(2)}) async-start(), calls=%async_computation.7 | async-start | bytes 2949120 | tf_op jit(solution)/shard_map/reduce_scatter | solution.py:25
  180.8 50.3 %all-to-all-start.3 = ((bf16[32,2,2,1280]{3,2,1,0:T(2,128)(2,1)}), bf16[32,2,2,1280]{3,2,1,0:T(2,128)(2,1)S(1)}, u32[]{:S(2)}, u32[]{:S(2)}) async-start(bf16[32,2,2,1280]{3,2,1,0:T(2,128)(2,1)} %copy.27), calls=%async_computation.5 | async-start | bytes 655360 | tf_op jit(solution)/shard_map/all_to_all | solution.py:28
  231.2 27.9 %all-to-all-start.1 = ((bf16[32,2,2,1280]{3,2,1,0:T(2,128)(2,1)}), bf16[32,2,2,1280]{3,2,1,0:T(2,128)(2,1)}, u32[]{:S(2)}, u32[]{:S(2)}) async-start(bf16[32,2,2,1280]{3,2,1,0:T(2,128)(2,1)} %copy.25), calls=%async_computation.2 | async-start | bytes 655360 | tf_op jit(solution)/shard_map/all_to_all | solution.py:28
  245.8 5.1 copy-start.1
  245.8 263.7 %all-reduce.2.cloned.1.call-start = ((), (), s32[]{:S(2)}) async-start(), calls=%async_computation.10 | async-start | bytes 1310720 | tf_op jit(solution)/shard_map/psum | solution.py:95
  260.2 1.7 copy-start.3
  261.8 0.7 copy-start.7
  261.8 0.7 copy-start.8
  261.9 0.7 copy-start.9
  263.8 2.3 copy-start.2
Sparse Core Ops, SparseCore 0:
  37.3 40.0 all-gather.2
  79.7 44.4 all-gather.4
  133.3 45.4 reduce-scatter.4
  181.2 47.8 reduce-scatter.2
  263.9 245.5 all-reduce.1
where the time goes:
time: 519 us; the launch traced here: 518 us
  waiting for transfers between devices  377 us (73%)
  blocking collectives  43.9 us (8%)
  matrix products  43 us (8%)
  starting transfers between devices  29.4 us (6%)
  between operations  14 us (3%)
  local copies, waits for them, and re-layouts  10.8 us (2%)
    psum x1, waiting for transfers between devices, per_device(): grad_router = lax.psum(router_term, ('dp', 'expert'))  241 us
    reduce_scatter x2, waiting for transfers between devices, from_experts(): lax.psum_scatter(held.astype(jnp.float32).astype(jnp.bfloat16), 'dp', sca...  70.1 us
    all_gather x2, waiting for transfers between devices, to_experts(): return lax.all_gather(moved, 'dp', axis=0, tiled=True)  59.2 us
    all_to_all x2, blocking collectives, to_experts(): lax.all_to_all(slot_block, 'expert', split_axis=0, concat_axis=0, tiled=T...  43.9 us
    all_to_all x2, starting transfers between devices, from_experts(): lax.all_to_all(summed, 'expert', split_axis=0, concat_axis=0, tiled=True)  29.1 us
  transfers between devices with their start and end apart: 7, of which 6 were waited for; matrix products, arithmetic and copies ran while one was open for 7% of the time, Pallas kernels for 0%

commit v1 on v0

v1 whole, which is shorter than its diff:
```python
import functools
import math

import jax
import jax.numpy as jnp
import numpy as np
from jax import lax
from jax.experimental import pallas as pl
from jax.experimental.pallas import tpu as pltpu
from jax.sharding import Mesh
from jax.sharding import PartitionSpec as P

F32 = jnp.float32
BF16 = jnp.bfloat16
ALL = ("xl", "y", "z", "xh", "c")
DP = ("xl", "y")
EXPERT = ("z", "xh", "c")
PLANE = ("xl", "y", "xh", "c")

PARTS = (((0, 0, 24),), ((1, 0, 24),), ((0, 24, 8), (1, 24, 8)))
ROWS = tuple(sum(4 * n for _, _, n in part) for part in PARTS)
ORDERS = (("x", "y1", "y3"), ("y1", "y3", "x"), ("y3", "x", "y1"))


def row_order():
    order = []
    for part in PARTS:
        for expert, first, count in part:
            for kind in range(2):
                for image in range(first, first + count):
                    for k in range(2):
                        order.append(8 * image + 4 * kind + 2 * expert + k)
    return np.array(order)


def neighbour(dim):
    pairs = []
    for i in range(8):
        x, y = divmod(i, 4)
        if dim == "x":
            x = 1 - x
        elif dim == "y1":
            y = y ^ 1
        else:
            y = 3 - y
        pairs.append((i, x * 4 + y))
    return pairs


def call(kernel, out_shape, args, flops, name):
    shapes = out_shape if isinstance(out_shape, tuple) else (out_shape,)
    moved = sum(math.prod(a.shape) * a.dtype.itemsize for a in tuple(args) + shapes)
    vmem = pl.BlockSpec(memory_space=pltpu.VMEM)
    return pl.pallas_call(
        kernel,
        out_shape=out_shape,
        in_specs=[vmem] * len(args),
        out_specs=(vmem,) * len(shapes) if isinstance(out_shape, tuple) else vmem,
        compiler_params=pltpu.CompilerParams(vmem_limit_bytes=48 * 1024 * 1024),
        cost_estimate=pl.CostEstimate(flops=flops, bytes_accessed=moved, transcendentals=0),
        name=name,
    )(*args)


def dot(a, b, over):
    return lax.dot_general(a, b, (over, ((), ())), preferred_element_type=F32)


PLAIN = ((1,), (0,))
WIDTH = ((1,), (1,))
FIRST = ((0,), (0,))


def spread(slots, wide):
    row = lax.broadcasted_iota(jnp.int32, (slots, wide), 0)
    col = lax.broadcasted_iota(jnp.int32, (slots, wide), 1)
    return (row == 4 * (col // 8) + col % 4).astype(BF16)


def input_columns(shape):
    return lax.broadcasted_iota(jnp.int32, shape, 1) % 8 < 4


def prologue_kernel(tokens, router, cotangent, rows, dispatch_out, combine_out):
    slots = router.shape[1]
    wide = 2 * slots
    router_wide = dot(router[...], spread(slots, wide), PLAIN).astype(BF16)
    logits = dot(tokens[...], router_wide, PLAIN)
    down = jnp.exp(logits - jnp.max(logits, axis=0, keepdims=True))
    dispatch = down / jnp.sum(down, axis=0, keepdims=True)
    across = jnp.exp(logits - jnp.max(logits, axis=1, keepdims=True))
    combine = across / (0.5 * jnp.sum(across, axis=1, keepdims=True))
    inputs = input_columns(logits.shape)
    dispatch_b = jnp.where(inputs, dispatch, 0.0).astype(BF16)
    combine_b = jnp.where(inputs, 0.0, combine).astype(BF16)
    total = dot(dispatch_b, tokens[...], FIRST) + dot(combine_b, cotangent[...], FIRST)
    rows[...] = total.astype(BF16)
    dispatch_out[...] = dispatch
    combine_out[...] = combine


def sort_kernel(order, rows, *parts):
    moved = dot(order[...], rows[...], PLAIN).astype(BF16)
    at = 0
    for part in parts:
        count = part.shape[0]
        part[...] = moved[at : at + count]
        at += count


def unsort_kernel(order, *refs):
    held, received, out = refs[:3], refs[3:6], refs[6]
    total = [
        (a[...].astype(F32) + b[...].astype(F32)).astype(BF16)
        for a, b in zip(held, received, strict=True)
    ]
    out[...] = dot(order[...], jnp.concatenate(total, axis=0), FIRST).astype(BF16)


def gelu_parts(v):
    cdf = 0.5 * (1.0 + lax.erf(v * math.sqrt(0.5)))
    slope = cdf + v * (jnp.exp(-0.5 * v * v) * (1.0 / math.sqrt(2.0 * math.pi)))
    return v * cdf, slope


def expert_kernel(part, blocks, expert_in, expert_out, out, act_out, hid_out):
    count = blocks.shape[0]
    width = blocks.shape[2]
    at = saved = 0
    for expert, _, images in part:
        half = 2 * images
        total = count * half
        rows = blocks[:, at : at + half, :].reshape(total, width)
        grads = blocks[:, at + half : at + 2 * half, :].reshape(total, width)
        hidden = dot(rows, expert_in[expert], PLAIN)
        grad_act = dot(grads, expert_out[expert], WIDTH)
        value, slope = gelu_parts(hidden)
        activated = value.astype(BF16)
        grad_hidden = (slope * grad_act).astype(BF16)
        slot_part = dot(activated, expert_out[expert], PLAIN).astype(BF16)
        grad_part = dot(grad_hidden, expert_in[expert], WIDTH).astype(BF16)
        out[:, at : at + half, :] = slot_part.reshape(count, half, width)
        out[:, at + half : at + 2 * half, :] = grad_part.reshape(count, half, width)
        act_out[saved : saved + total, :] = activated
        hid_out[saved : saved + total, :] = grad_hidden
        at += 2 * half
        saved += total


def weight_kernel(sections, kind, *refs):
    out = refs[-1]
    left, right = [], []
    for i, (at, half, first) in enumerate(sections):
        blocks, saved = refs[2 * i], refs[2 * i + 1]
        total = blocks.shape[0] * half
        left.append(blocks[:, at : at + half, :].reshape(total, blocks.shape[2]))
        right.append(saved[first : first + total, :])
    left = jnp.concatenate(left, axis=0)
    right = jnp.concatenate(right, axis=0)
    if kind == "in":
        out[...] = dot(left, right, FIRST).astype(BF16)
    else:
        out[...] = dot(right, left, FIRST).astype(BF16)


def router_kernel(tokens, cotangent, rows, dispatch_in, combine_in, term, grad_logits_out):
    slots = grad_logits_out.shape[1]
    wide = 2 * slots
    dispatch, combine = dispatch_in[...], combine_in[...]
    inputs = input_columns(dispatch.shape)
    grad_combine = jnp.where(inputs, dot(cotangent[...], rows[...], WIDTH), 0.0)
    grad_dispatch = dot(tokens[...], rows[...], WIDTH)
    logit_combine = combine * (
        grad_combine - jnp.sum(combine * grad_combine, axis=1, keepdims=True)
    )
    logit_dispatch = dispatch * (
        grad_dispatch - jnp.sum(dispatch * grad_dispatch, axis=0, keepdims=True)
    )
    both = logit_combine + pltpu.roll(logit_dispatch, wide - 4, 1)
    both = jnp.where(inputs, both, 0.0).astype(BF16)
    grad_logits = dot(both, spread(slots, wide), WIDTH).astype(BF16)
    grad_logits_out[...] = grad_logits
    term[...] = dot(tokens[...], grad_logits, FIRST).astype(BF16)


def tokens_kernel(rows, router, dispatch_in, combine_in, grad_logits, mixed, grad_tokens):
    inputs = input_columns(dispatch_in.shape)
    combine_b = jnp.where(inputs, combine_in[...], 0.0).astype(BF16)
    dispatch_b = jnp.where(inputs, 0.0, dispatch_in[...]).astype(BF16)
    mixed[...] = dot(combine_b, rows[...], PLAIN).astype(BF16)
    through = dot(dispatch_b, rows[...], PLAIN) + dot(grad_logits[...], router[...], WIDTH)
    grad_tokens[...] = through.astype(BF16)


def shape(dims, dtype=BF16):
    return jax.ShapeDtypeStruct(dims, dtype)


def swap(value, axis):
    return lax.all_to_all(value, axis, split_axis=0, concat_axis=0, tiled=True)


def sum_router(term):
    slots = term.shape[1]
    n_plane = lax.axis_size(PLANE)
    n_z = lax.axis_size("z")
    share = swap(term.reshape(n_plane, term.shape[0] // n_plane, slots), PLANE)
    share = jnp.sum(share.astype(F32), axis=0).astype(BF16)
    share = swap(jnp.broadcast_to(share[None], (n_z,) + share.shape), "z")
    share = jnp.sum(share.astype(F32), axis=0).astype(BF16)
    full = swap(jnp.broadcast_to(share[None], (n_plane,) + share.shape), PLANE)
    return full.reshape(term.shape).astype(F32)


def per_device(tokens, router, expert_in, expert_out, cotangent):
    n_expert = lax.axis_size(EXPERT)
    count, width = tokens.shape
    slots = router.shape[1]
    wide = 2 * slots
    hidden_units = expert_in.shape[2]
    order = np.zeros((wide, wide), np.float32)
    order[np.arange(wide), row_order()] = 1.0
    order = jnp.asarray(order, BF16)

    rows, dispatch, combine = call(
        prologue_kernel,
        (shape((wide, width)), shape((count, wide), F32), shape((count, wide), F32)),
        (tokens, router, cotangent),
        6 * count * wide * width,
        "prologue",
    )
    rows = swap(rows.reshape(n_expert, 8, width), EXPERT).reshape(wide, width)
    parts = call(
        sort_kernel,
        tuple(shape((n, width)) for n in ROWS),
        (order, rows),
        2 * wide * wide * width,
        "sort",
    )

    near = [part[None] for part in parts]
    far = None
    for step in range(3):
        far = [
            lax.ppermute(near[p], DP, neighbour(ORDERS[p][step])) for p in range(len(PARTS))
        ]
        if step < 2:
            near = [jnp.concatenate([a, b], axis=0) for a, b in zip(near, far, strict=True)]

    def experts(p, blocks):
        n = blocks.shape[0]
        kept = shape((n * ROWS[p] // 2, hidden_units))
        return call(
            functools.partial(expert_kernel, PARTS[p]),
            (shape(blocks.shape), kept, kept),
            (blocks, expert_in, expert_out),
            4 * n * ROWS[p] * width * hidden_units,
            f"experts{p}",
        )

    near_done = [experts(p, near[p]) for p in range(len(PARTS))]
    far_done = [experts(p, far[p]) for p in range(len(PARTS))]

    sums = [done[0] for done in near_done]
    leaving = [done[0] for done in far_done]
    for step in (2, 1, 0):
        arrived = [
            lax.ppermute(leaving[p], DP, neighbour(ORDERS[p][step])) for p in range(len(PARTS))
        ]
        if step > 0:
            sums = [
                (a.astype(F32) + b.astype(F32)).astype(BF16)
                for a, b in zip(sums, arrived, strict=True)
            ]
            half = sums[0].shape[0] // 2
            leaving = [s[half:] for s in sums]
            sums = [s[:half] for s in sums]

    def weights(expert, kind):
        sections, args = [], []
        for p, part in enumerate(PARTS):
            for blocks, done in ((near[p], near_done[p]), (far[p], far_done[p])):
                at = saved = 0
                for owner, _, images in part:
                    half = 2 * images
                    if owner == expert:
                        sections.append((at + (0 if kind == "in" else half), half, saved))
                        args += [blocks, done[2 if kind == "in" else 1]]
                    at += 2 * half
                    saved += blocks.shape[0] * half
        dims = (width, hidden_units) if kind == "in" else (hidden_units, width)
        return call(
            functools.partial(weight_kernel, tuple(sections), kind),
            shape(dims),
            tuple(args),
            2 * 512 * width * hidden_units,
            f"weights_{kind}{expert}",
        )

    grad_in = jnp.stack([weights(0, "in"), weights(1, "in")])
    grad_out = jnp.stack([weights(0, "out"), weights(1, "out")])

    back = call(
        unsort_kernel,
        shape((wide, width)),
        (order, *(s[0] for s in sums), *(a[0] for a in arrived)),
        2 * wide * wide * width,
        "unsort",
    )
    back = swap(back.reshape(n_expert, 8, width), EXPERT).reshape(wide, width)
    term, grad_logits = call(
        router_kernel,
        (shape((width, slots)), shape((count, slots))),
        (tokens, cotangent, back, dispatch, combine),
        6 * count * wide * width,
        "router_gradient",
    )
    mixed, grad_tokens = call(
        tokens_kernel,
        (shape((count, width)), shape((count, width))),
        (back, router, dispatch, combine, grad_logits),
        5 * count * wide * width,
        "token_outputs",
    )
    return (mixed, grad_tokens, sum_router(term), grad_in, grad_out)


def solution(mesh):
    grid = Mesh(mesh.devices.reshape(2, 4, 8, 2, 2), ALL)
    in_specs = (
        P(ALL, None),
        P(),
        P(EXPERT, None, DP),
        P(EXPERT, DP, None),
        P(ALL, None),
    )
    out_specs = (
        P(ALL, None),
        P(ALL, None),
        P(),
        P(EXPERT, None, DP),
        P(EXPERT, DP, None),
    )
    return jax.shard_map(
        per_device, mesh=grid, in_specs=in_specs, out_specs=out_specs, check_vma=False
    )
```

time: 519 us -> 242 us (0.47)
  waiting for transfers between devices: 377 us -> 70 us
  matrix products: 43 us -> 0 us
  blocking collectives: 43.9 us -> 76.4 us
  starting transfers between devices: 29.4 us -> 48.1 us
  Pallas kernels: 0 us -> 17 us
  between operations: 14 us -> 1.33 us
  other arithmetic: 0.19 us -> 9.97 us
  local copies, waits for them, and re-layouts: 10.8 us -> 18.3 us
    psum x1 -> x0, waiting for transfers between devices: 241 us -> none  [per_device(): grad_router = lax.psum(router_term, ('dp', 'expert'))]
    reduce_scatter x2 -> x0, waiting for transfers between devices: 70.1 us -> none  [from_experts(): lax.psum_scatter(held.astype(jnp.float32).astype(jnp.bfloat16), 'dp', sca...]
    ppermute x0 -> x18, waiting for transfers between devices: none -> 63.3 us  [the longest x9 32.5 us: per_device(): lax.ppermute(near[p], DP, neighbour(ORDERS[p][step]))]
    all_gather x2 -> x0, waiting for transfers between devices: 59.2 us -> none  [to_experts(): return lax.all_gather(moved, 'dp', axis=0, tiled=True)]
    dot_general x15 -> x0, matrix products: 43 us -> none  [the longest x1 8.14 us: per_device(): jnp.einsum('rjkd,jdf->rjkf', gathered, expert_in, preferred_element_type=...]
    all_to_all x2, blocking collectives: 43.9 us -> 76.4 us  [swap(): return lax.all_to_all(value, axis, split_axis=0, concat_axis=0, tiled=True)]
    ppermute x0 -> x18, starting transfers between devices: none -> 27.3 us  [the longest x9 15.8 us: per_device(): lax.ppermute(leaving[p], DP, neighbour(ORDERS[p][step]))]
    pallas_call x0 -> x15, Pallas kernels: none -> 17 us  [call(): pl.pallas_call(kernel, out_shape=out_shape, in_specs=[vmem] * len(args),...]
  transfers between devices with their start and end apart: 7 -> 21, of which waited for: 6 -> 16; matrix products, arithmetic and copies ran while one was open for 7% -> 3% of each run, Pallas kernels for 0% -> 6%
where the time goes in v1:
time: 242 us; the launch traced here: 241 us
  blocking collectives  76.4 us (32%)
  waiting for transfers between devices  70 us (29%)
  starting transfers between devices  48.1 us (20%)
  local copies, waits for them, and re-layouts  18.3 us (8%)
  Pallas kernels  17 us (7%)
  other arithmetic  9.97 us (4%)
    all_to_all x2, blocking collectives, swap(): return lax.all_to_all(value, axis, split_axis=0, concat_axis=0, tiled=True)  76.4 us
    ppermute x9, waiting for transfers between devices, per_device(): lax.ppermute(near[p], DP, neighbour(ORDERS[p][step]))  32.5 us
    ppermute x9, waiting for transfers between devices, per_device(): lax.ppermute(leaving[p], DP, neighbour(ORDERS[p][step]))  30.8 us
    all_to_all x3, starting transfers between devices, swap(): return lax.all_to_all(value, axis, split_axis=0, concat_axis=0, tiled=True)  20.8 us
    pallas_call x15, Pallas kernels, call(): pl.pallas_call(kernel, out_shape=out_shape, in_specs=[vmem] * len(args),...  17 us
    unnamed x102, local copies, waits for them, and re-layouts  16.7 us
    ppermute x9, starting transfers between devices, per_device(): lax.ppermute(leaving[p], DP, neighbour(ORDERS[p][step]))  15.8 us
    ppermute x9, starting transfers between devices, per_device(): lax.ppermute(near[p], DP, neighbour(ORDERS[p][step]))  11.5 us
  transfers between devices with their start and end apart: 21, of which 16 were waited for; matrix products, arithmetic and copies ran while one was open for 3% of the time, Pallas kernels for 6%

profile of v1, /device:TPU:1, one launch (start us, length us, event | category | flops | bytes accessed | tf_op | source)
XLA Modules:
  0.0 241.0 jit_solution(2753499025149813359)
XLA Ops:
  5.2 32.3 %all_to_all.25 = bf16[32,8,1280]{2,1,0:T(8,128)(2,1)S(1)} all-to-all(bf16[32,8,1280]{2,1,0:T(8,128)(2,1)S(1)} %bitcast.41), channel_id=1, replica_groups=mesh['xl'=2,'y'=4,'z'=8,'xh'=2,'c'=2] {'z','xh','c'}, dimensions={0} | all-to-all | bytes 1310720 | tf_op jit(solution)/shard_map/all_to_all | solution.py:200
  37.9 2.8 %collective-permute-start.10 = (bf16[1,64,1280]{2,1,0:T(8,128)(2,1)S(1)}, bf16[1,64,1280]{2,1,0:T(8,128)(2,1)S(1)}, u32[]{:S(2)}, u32[]{:S(2)}) collective-permute-start(bf16[1,64,1280]{2,1,0:T(8,128)(2,1)S(1)} %bitcast.38), channel_id=1, source_target_pairs={{0,96},{32,64},{64,32},{96,0},{128,224},{160,192},{192,160},{224,1... | collective-permute-start | bytes 491528 | tf_op jit(solution)/shard_map/ppermute | solution.py:245
  41.0 2.9 %collective-permute-done.10 = bf16[1,64,1280]{2,1,0:T(8,128)(2,1)S(1)} collective-permute-done((bf16[1,64,1280]{2,1,0:T(8,128)(2,1)S(1)}, bf16[1,64,1280]{2,1,0:T(8,128)(2,1)S(1)}, u32[]{:S(2)}, u32[]{:S(2)}) %collective-permute-start.10) | collective-permute-done | bytes 163872 | tf_op jit(solution)/shard_map/ppermute | solution.py:245
  44.4 2.4 %collective-permute-done = bf16[1,96,1280]{2,1,0:T(8,128)(2,1)S(1)} collective-permute-done((bf16[1,96,1280]{2,1,0:T(8,128)(2,1)S(1)}, bf16[1,96,1280]{2,1,0:T(8,128)(2,1)S(1)}, u32[]{:S(2)}, u32[]{:S(2)}) %collective-permute-start) | collective-permute-done | bytes 245792 | tf_op jit(solution)/shard_map/ppermute | solution.py:245
  48.4 5.4 %collective-permute-done.11 = bf16[2,64,1280]{2,1,0:T(8,128)(2,1)S(1)} collective-permute-done((bf16[2,64,1280]{2,1,0:T(8,128)(2,1)S(1)}, bf16[2,64,1280]{2,1,0:T(8,128)(2,1)S(1)}, u32[]{:S(2)}, u32[]{:S(2)}) %collective-permute-start.11) | collective-permute-done | bytes 327712 | tf_op jit(solution)/shard_map/ppermute | solution.py:245
  54.0 1.6 collective-permute-done.1
  55.7 2.3 collective-permute-start.2
  57.9 2.9 %collective-permute-done.5 = bf16[1,96,1280]{2,1,0:T(8,128)(2,1)S(1)} collective-permute-done((bf16[1,96,1280]{2,1,0:T(8,128)(2,1)S(1)}, bf16[1,96,1280]{2,1,0:T(8,128)(2,1)S(1)}, u32[]{:S(2)}, u32[]{:S(2)}) %collective-permute-start.5) | collective-permute-done | bytes 245792 | tf_op jit(solution)/shard_map/ppermute | solution.py:245
  60.9 2.3 collective-permute-start.6
  63.1 11.7 %collective-permute-done.12.blocks.refs_6_ = bf16[4,64,1280]{2,1,0:T(8,128)(2,1)S(1)} collective-permute-done((bf16[4,64,1280]{2,1,0:T(8,128)(2,1)S(1)}, bf16[4,64,1280]{2,1,0:T(8,128)(2,1)S(1)}, u32[]{:S(2)}, u32[]{:S(2)}) %collective-permute-start.12) | collective-permute-done | bytes 655392 | tf_op jit(solution)/shard_map/ppermute | solution.py:245
  74.9 1.9 experts2.3
  78.3 3.9 %collective-permute-done.6 = bf16[2,96,1280]{2,1,0:T(8,128)(2,1)S(1)} collective-permute-done((bf16[2,96,1280]{2,1,0:T(8,128)(2,1)S(1)}, bf16[2,96,1280]{2,1,0:T(8,128)(2,1)S(1)}, u32[]{:S(2)}, u32[]{:S(2)}) %collective-permute-start.6) | collective-permute-done | bytes 491552 | tf_op jit(solution)/shard_map/ppermute | solution.py:245
  82.4 1.8 collective-permute-start.7
  84.2 1.9 experts2.2
  87.5 3.7 %collective-permute-start.3 = (bf16[4,96,1280]{2,1,0:T(8,128)(2,1)S(1)}, bf16[4,96,1280]{2,1,0:T(8,128)(2,1)S(1)}, u32[]{:S(2)}, u32[]{:S(2)}) collective-permute-start(bf16[4,96,1280]{2,1,0:T(8,128)(2,1)S(1)} %get-tuple-element.36), channel_id=1, source_target_pairs={{0,96},{32,64},{64,32},{96,0},{128,224},{160,192},{192,160},{224,1... | collective-permute-start | bytes 2949128 | tf_op jit(solution)/shard_map/ppermute | solution.py:268
  95.4 1.6 collective-permute-done.7.blocks.refs_2_
  98.4 2.3 collective-permute-start.8
  100.7 3.4 %collective-permute-done.14 = bf16[2,64,1280]{2,1,0:T(8,128)(2,1)S(1)} collective-permute-done((bf16[2,64,1280]{2,1,0:T(8,128)(2,1)S(1)}, bf16[2,64,1280]{2,1,0:T(8,128)(2,1)S(1)}, u32[]{:S(2)}, u32[]{:S(2)}) %collective-permute-start.14) | collective-permute-done | bytes 327712 | tf_op jit(solution)/shard_map/ppermute | solution.py:268
  105.6 19.5 %collective-permute-done.8 = bf16[4,96,1280]{2,1,0:T(8,128)(2,1)S(1)} collective-permute-done((bf16[4,96,1280]{2,1,0:T(8,128)(2,1)S(1)}, bf16[4,96,1280]{2,1,0:T(8,128)(2,1)S(1)}, u32[]{:S(2)}, u32[]{:S(2)}) %collective-permute-start.8) | collective-permute-done | bytes 983072 | tf_op jit(solution)/shard_map/ppermute | solution.py:268
  125.4 4.5 %collective-permute-start.9 = (bf16[2,96,1280]{2,1,0:T(8,128)(2,1)S(1)}, bf16[2,96,1280]{2,1,0:T(8,128)(2,1)S(1)}, u32[]{:S(2)}, u32[]{:S(2)}) collective-permute-start(bf16[2,96,1280]{2,1,0:T(8,128)(2,1)S(1)} %slice.52), channel_id=1, source_target_pairs={{0,96},{32,64},{64,32},{96,0},{128,224},{160,192},{192,160},{224,1... | collective-permute-start | bytes 1474568 | tf_op jit(solution)/shard_map/ppermute | solution.py:268
  130.1 2.0 collective-permute-start.15
  132.1 4.1 %collective-permute-done.9 = bf16[2,96,1280]{2,1,0:T(8,128)(2,1)S(1)} collective-permute-done((bf16[2,96,1280]{2,1,0:T(8,128)(2,1)S(1)}, bf16[2,96,1280]{2,1,0:T(8,128)(2,1)S(1)}, u32[]{:S(2)}, u32[]{:S(2)}) %collective-permute-start.9) | collective-permute-done | bytes 491552 | tf_op jit(solution)/shard_map/ppermute | solution.py:268
  136.4 2.8 %collective-permute-start.17 = (bf16[1,64,1280]{2,1,0:T(8,128)(2,1)S(1)}, bf16[1,64,1280]{2,1,0:T(8,128)(2,1)S(1)}, u32[]{:S(2)}, u32[]{:S(2)}) collective-permute-start(bf16[1,64,1280]{2,1,0:T(8,128)(2,1)S(1)} %get-tuple-element.65), channel_id=1, source_target_pairs={{0,96},{32,64},{64,32},{96,0},{128,224},{160,192},{192,160},{224,1... | collective-permute-start | bytes 491528 | tf_op jit(solution)/shard_map/ppermute | solution.py:268
  139.2 2.7 %collective-permute-done.17 = bf16[1,64,1280]{2,1,0:T(8,128)(2,1)S(1)} collective-permute-done((bf16[1,64,1280]{2,1,0:T(8,128)(2,1)S(1)}, bf16[1,64,1280]{2,1,0:T(8,128)(2,1)S(1)}, u32[]{:S(2)}, u32[]{:S(2)}) %collective-permute-start.17) | collective-permute-done | bytes 163872 | tf_op jit(solution)/shard_map/ppermute | solution.py:268
  142.3 44.1 %all_to_all.26 = bf16[32,8,1280]{2,1,0:T(8,128)(2,1)S(1)} all-to-all(bf16[32,8,1280]{2,1,0:T(8,128)(2,1)S(1)} %bitcast.30), channel_id=1, replica_groups=mesh['xl'=2,'y'=4,'z'=8,'xh'=2,'c'=2] {'z','xh','c'}, dimensions={0} | all-to-all | bytes 1310720 | tf_op jit(solution)/shard_map/all_to_all | solution.py:200
  189.8 9.1 %all-to-all-start.2 = ((bf16[32,40,128]{2,1,0:T(8,128)(2,1)}), bf16[32,40,128]{2,1,0:T(8,128)(2,1)}, u32[]{:S(2)}, u32[]{:S(2)}) async-start(bf16[32,40,128]{2,1,0:T(8,128)(2,1)} %bitcast.42), calls=%async_computation.2 | async-start | bytes 655360 | tf_op jit(solution)/shard_map/all_to_all | solution.py:200
  210.1 4.2 %all-to-all-start.3 = ((bf16[8,40,128]{2,1,0:T(8,128)(2,1)}), bf16[8,40,128]{2,1,0:T(8,128)(2,1)}, u32[]{:S(2)}, u32[]{:S(2)}) async-start(bf16[8,40,128]{2,1,0:T(8,128)(2,1)} %broadcast_in_dim.24), calls=%async_computation.3 | async-start | bytes 163840 | tf_op jit(solution)/shard_map/all_to_all | solution.py:200
  214.3 3.1 %pad_maximum_fusion.1 = bf16[2,384,1280]{2,1,0:T(8,128)(2,1)} fusion(bf16[1,384,1280]{2,1,0:T(8,128)(2,1)} %bitcast.29, bf16[1,384,1280]{2,1,0:T(8,128)(2,1)} %bitcast.28), kind=kLoop, calls=%fused_computation.1 | loop fusion | flops 983040 | bytes 3932160 | tf_op jit(solution)/shard_map/stack | solution.py:301
  223.2 7.5 %all-to-all-start.4 = ((bf16[32,40,128]{2,1,0:T(8,128)(2,1)}), bf16[32,40,128]{2,1,0:T(8,128)(2,1)S(1)}, u32[]{:S(2)}, u32[]{:S(2)}) async-start(bf16[32,40,128]{2,1,0:T(8,128)(2,1)} %broadcast_in_dim.25), calls=%async_computation.4 | async-start | bytes 655360 | tf_op jit(solution)/shard_map/all_to_all | solution.py:200
  230.8 2.8 %pad_maximum_fusion = bf16[2,1280,384]{2,1,0:T(8,128)(2,1)} fusion(bf16[1,1280,384]{2,1,0:T(8,128)(2,1)} %bitcast.27, bf16[1,1280,384]{2,1,0:T(8,128)(2,1)S(1)} %bitcast.26), kind=kLoop, calls=%fused_computation | loop fusion | flops 983040 | bytes 3932160 | tf_op jit(solution)/shard_map/stack | solution.py:300
  233.6 1.5 token_outputs.1
  235.1 5.1 %all-to-all-done.4 = bf16[32,40,128]{2,1,0:T(8,128)(2,1)S(1)} async-done(((bf16[32,40,128]{2,1,0:T(8,128)(2,1)}), bf16[32,40,128]{2,1,0:T(8,128)(2,1)S(1)}, u32[]{:S(2)}, u32[]{:S(2)}) %all-to-all-start.4) | async-done | bytes 327712 | tf_op jit(solution)/shard_map/all_to_all | solution.py:200
  (154 shorter events, 39.8 us)
Async XLA Ops:
  3.8 33.7 %copy-start.21 = (bf16[256,256]{1,0:T(8,128)(2,1)S(1)}, bf16[256,256]{1,0:T(8,128)(2,1)}, u32[]{:S(2)}) copy-start(bf16[256,256]{1,0:T(8,128)(2,1)} %constant.6.clone.order) | copy-start | bytes 393220
  5.2 181.2 %copy-start.15 = (f32[256,256]{1,0:T(8,128)}, f32[256,256]{1,0:T(8,128)S(1)}, u32[]{:S(2)}) copy-start(f32[256,256]{1,0:T(8,128)S(1)} %get-tuple-element.44.combine_in) | copy-start | bytes 786436
  37.9 6.1 %collective-permute-start.10 = (bf16[1,64,1280]{2,1,0:T(8,128)(2,1)S(1)}, bf16[1,64,1280]{2,1,0:T(8,128)(2,1)S(1)}, u32[]{:S(2)}, u32[]{:S(2)}) collective-permute-start(bf16[1,64,1280]{2,1,0:T(8,128)(2,1)S(1)} %bitcast.38), channel_id=1, source_target_pairs={{0,96},{32,64},{64,32},{96,0},{128,224},{160,192},{192,160},{224,1... | collective-permute-start | bytes 491528 | tf_op jit(solution)/shard_map/ppermute | solution.py:245
  40.7 6.1 %collective-permute-start = (bf16[1,96,1280]{2,1,0:T(8,128)(2,1)S(1)}, bf16[1,96,1280]{2,1,0:T(8,128)(2,1)S(1)}, u32[]{:S(2)}, u32[]{:S(2)}) collective-permute-start(bf16[1,96,1280]{2,1,0:T(8,128)(2,1)S(1)} %bitcast.35), channel_id=1, source_target_pairs={{0,128},{32,160},{64,192},{96,224},{128,0},{160,32},{192,64},{224,... | collective-permute-start | bytes 737288 | tf_op jit(solution)/shard_map/ppermute | solution.py:245
  44.0 9.9 %collective-permute-start.11 = (bf16[2,64,1280]{2,1,0:T(8,128)(2,1)S(1)}, bf16[2,64,1280]{2,1,0:T(8,128)(2,1)S(1)}, u32[]{:S(2)}, u32[]{:S(2)}) collective-permute-start(bf16[2,64,1280]{2,1,0:T(8,128)(2,1)S(1)} %pad_maximum_fusion.7), channel_id=1, source_target_pairs={{0,128},{32,160},{64,192},{96,224},{128,0},{160,32},{192,64},{224,... | collective-permute-start | bytes 983048 | tf_op jit(solution)/shard_map/ppermute | solution.py:245
  46.9 8.7 %collective-permute-start.1 = (bf16[2,96,1280]{2,1,0:T(8,128)(2,1)S(1)}, bf16[2,96,1280]{2,1,0:T(8,128)(2,1)S(1)}, u32[]{:S(2)}, u32[]{:S(2)}) collective-permute-start(bf16[2,96,1280]{2,1,0:T(8,128)(2,1)S(1)} %pad_maximum_fusion.5), channel_id=1, source_target_pairs={{0,32},{32,0},{64,96},{96,64},{128,160},{160,128},{192,224},{224,1... | collective-permute-start | bytes 1474568 | tf_op jit(solution)/shard_map/ppermute | solution.py:245
  47.0 27.9 %copy-start = (bf16[2,1280,384]{2,1,0:T(8,128)(2,1)S(1)}, bf16[2,1280,384]{2,1,0:T(8,128)(2,1)}, u32[]{:S(2)}) copy-start(bf16[2,1280,384]{2,1,0:T(8,128)(2,1)} %expert_in.11) | copy-start | bytes 5898244
  47.0 27.9 %copy-start.1 = (bf16[2,384,1280]{2,1,0:T(8,128)(2,1)S(1)}, bf16[2,384,1280]{2,1,0:T(8,128)(2,1)}, u32[]{:S(2)}) copy-start(bf16[2,384,1280]{2,1,0:T(8,128)(2,1)} %expert_out.11) | copy-start | bytes 5898244
  47.0 13.8 %collective-permute-start.5 = (bf16[1,96,1280]{2,1,0:T(8,128)(2,1)S(1)}, bf16[1,96,1280]{2,1,0:T(8,128)(2,1)S(1)}, u32[]{:S(2)}, u32[]{:S(2)}) collective-permute-start(bf16[1,96,1280]{2,1,0:T(8,128)(2,1)S(1)} %bitcast.32), channel_id=1, source_target_pairs={{0,32},{32,0},{64,96},{96,64},{128,160},{160,128},{192,224},{224,1... | collective-permute-start | bytes 737288 | tf_op jit(solution)/shard_map/ppermute | solution.py:245
  53.9 21.0 %collective-permute-start.12 = (bf16[4,64,1280]{2,1,0:T(8,128)(2,1)S(1)}, bf16[4,64,1280]{2,1,0:T(8,128)(2,1)S(1)}, u32[]{:S(2)}, u32[]{:S(2)}) collective-permute-start(bf16[4,64,1280]{2,1,0:T(8,128)(2,1)S(1)} %pad_maximum_fusion.4.blocks.refs_4_), channel_id=1, source_target_pairs={{0,32},{32,0},{64,96},{96,64},{128,160},{160,128},{192,224},{224,1... | collective-permute-start | bytes 1966088 | tf_op jit(solution)/shard_map/ppermute | solution.py:245
  55.7 30.4 %collective-permute-start.2 = (bf16[4,96,1280]{2,1,0:T(8,128)(2,1)S(1)}, bf16[4,96,1280]{2,1,0:T(8,128)(2,1)S(1)}, u32[]{:S(2)}, u32[]{:S(2)}) collective-permute-start(bf16[4,96,1280]{2,1,0:T(8,128)(2,1)S(1)} %pad_maximum_fusion.2.blocks.refs_0_), channel_id=1, source_target_pairs={{0,96},{32,64},{64,32},{96,0},{128,224},{160,192},{192,160},{224,1... | collective-permute-start | bytes 2949128 | tf_op jit(solution)/shard_map/ppermute | solution.py:245
  60.9 21.4 %collective-permute-start.6 = (bf16[2,96,1280]{2,1,0:T(8,128)(2,1)S(1)}, bf16[2,96,1280]{2,1,0:T(8,128)(2,1)S(1)}, u32[]{:S(2)}, u32[]{:S(2)}) collective-permute-start(bf16[2,96,1280]{2,1,0:T(8,128)(2,1)S(1)} %pad_maximum_fusion.6), channel_id=1, source_target_pairs={{0,96},{32,64},{64,32},{96,0},{128,224},{160,192},{192,160},{224,1... | collective-permute-start | bytes 1474568 | tf_op jit(solution)/shard_map/ppermute | solution.py:245
  78.1 13.1 %collective-permute-start.13 = (bf16[4,64,1280]{2,1,0:T(8,128)(2,1)S(1)}, bf16[4,64,1280]{2,1,0:T(8,128)(2,1)S(1)}, u32[]{:S(2)}, u32[]{:S(2)}) collective-permute-start(bf16[4,64,1280]{2,1,0:T(8,128)(2,1)S(1)} %get-tuple-element.42), channel_id=1, source_target_pairs={{0,32},{32,0},{64,96},{96,64},{128,160},{160,128},{192,224},{224,1... | collective-permute-start | bytes 1966088 | tf_op jit(solution)/shard_map/ppermute | solution.py:268
  82.4 14.6 %collective-permute-start.7 = (bf16[4,96,1280]{2,1,0:T(8,128)(2,1)S(1)}, bf16[4,96,1280]{2,1,0:T(8,128)(2,1)S(1)}, u32[]{:S(2)}, u32[]{:S(2)}) collective-permute-start(bf16[4,96,1280]{2,1,0:T(8,128)(2,1)S(1)} %pad_maximum_fusion.3.blocks.refs_0_), channel_id=1, source_target_pairs={{0,128},{32,160},{64,192},{96,224},{128,0},{160,32},{192,64},{224,... | collective-permute-start | bytes 2949128 | tf_op jit(solution)/shard_map/ppermute | solution.py:245
  87.4 4.0 %copy-start.33 = (bf16[192,384]{1,0:T(8,128)(2,1)}, bf16[192,384]{1,0:T(8,128)(2,1)S(1)}, u32[]{:S(2)}) copy-start(bf16[192,384]{1,0:T(8,128)(2,1)S(1)} %get-tuple-element.50.refs_3_) | copy-start | bytes 442372
  87.4 4.0 %copy-start.41 = (bf16[192,384]{1,0:T(8,128)(2,1)}, bf16[192,384]{1,0:T(8,128)(2,1)S(1)}, u32[]{:S(2)}) copy-start(bf16[192,384]{1,0:T(8,128)(2,1)S(1)} %get-tuple-element.56.refs_3_) | copy-start | bytes 442372
  87.5 17.7 %collective-permute-start.3 = (bf16[4,96,1280]{2,1,0:T(8,128)(2,1)S(1)}, bf16[4,96,1280]{2,1,0:T(8,128)(2,1)S(1)}, u32[]{:S(2)}, u32[]{:S(2)}) collective-permute-start(bf16[4,96,1280]{2,1,0:T(8,128)(2,1)S(1)} %get-tuple-element.36), channel_id=1, source_target_pairs={{0,96},{32,64},{64,32},{96,0},{128,224},{160,192},{192,160},{224,1... | collective-permute-start | bytes 2949128 | tf_op jit(solution)/shard_map/ppermute | solution.py:268
  91.3 12.7 %collective-permute-start.14 = (bf16[2,64,1280]{2,1,0:T(8,128)(2,1)S(1)}, bf16[2,64,1280]{2,1,0:T(8,128)(2,1)S(1)}, u32[]{:S(2)}, u32[]{:S(2)}) collective-permute-start(bf16[2,64,1280]{2,1,0:T(8,128)(2,1)S(1)} %slice.55), channel_id=1, source_target_pairs={{0,128},{32,160},{64,192},{96,224},{128,0},{160,32},{192,64},{224,... | collective-permute-start | bytes 983048 | tf_op jit(solution)/shard_map/ppermute | solution.py:268
  98.3 7.1 %copy-start.39 = (bf16[192,384]{1,0:T(8,128)(2,1)}, bf16[192,384]{1,0:T(8,128)(2,1)S(1)}, u32[]{:S(2)}) copy-start(bf16[192,384]{1,0:T(8,128)(2,1)S(1)} %get-tuple-element.54.refs_3_) | copy-start | bytes 442372
  98.4 7.1 %copy-start.47 = (bf16[192,384]{1,0:T(8,128)(2,1)}, bf16[192,384]{1,0:T(8,128)(2,1)S(1)}, u32[]{:S(2)}) copy-start(bf16[192,384]{1,0:T(8,128)(2,1)S(1)} %get-tuple-element.60.refs_3_) | copy-start | bytes 442372
  98.4 26.8 %collective-permute-start.8 = (bf16[4,96,1280]{2,1,0:T(8,128)(2,1)S(1)}, bf16[4,96,1280]{2,1,0:T(8,128)(2,1)S(1)}, u32[]{:S(2)}, u32[]{:S(2)}) collective-permute-start(bf16[4,96,1280]{2,1,0:T(8,128)(2,1)S(1)} %get-tuple-element.39), channel_id=1, source_target_pairs={{0,128},{32,160},{64,192},{96,224},{128,0},{160,32},{192,64},{224,... | collective-permute-start | bytes 2949128 | tf_op jit(solution)/shard_map/ppermute | solution.py:268
  105.5 24.4 %collective-permute-start.4 = (bf16[2,96,1280]{2,1,0:T(8,128)(2,1)S(1)}, bf16[2,96,1280]{2,1,0:T(8,128)(2,1)S(1)}, u32[]{:S(2)}, u32[]{:S(2)}) collective-permute-start(bf16[2,96,1280]{2,1,0:T(8,128)(2,1)S(1)} %slice.49), channel_id=1, source_target_pairs={{0,32},{32,0},{64,96},{96,64},{128,160},{160,128},{192,224},{224,1... | collective-permute-start | bytes 1474568 | tf_op jit(solution)/shard_map/ppermute | solution.py:268
  125.4 10.7 %collective-permute-start.9 = (bf16[2,96,1280]{2,1,0:T(8,128)(2,1)S(1)}, bf16[2,96,1280]{2,1,0:T(8,128)(2,1)S(1)}, u32[]{:S(2)}, u32[]{:S(2)}) collective-permute-start(bf16[2,96,1280]{2,1,0:T(8,128)(2,1)S(1)} %slice.52), channel_id=1, source_target_pairs={{0,96},{32,64},{64,32},{96,0},{128,224},{160,192},{192,160},{224,1... | collective-permute-start | bytes 1474568 | tf_op jit(solution)/shard_map/ppermute | solution.py:268
  130.1 11.8 %collective-permute-start.15 = (bf16[1,96,1280]{2,1,0:T(8,128)(2,1)S(1)}, bf16[1,96,1280]{2,1,0:T(8,128)(2,1)S(1)}, u32[]{:S(2)}, u32[]{:S(2)}) collective-permute-start(bf16[1,96,1280]{2,1,0:T(8,128)(2,1)S(1)} %get-tuple-element.63), channel_id=1, source_target_pairs={{0,128},{32,160},{64,192},{96,224},{128,0},{160,32},{192,64},{224,... | collective-permute-start | bytes 737288 | tf_op jit(solution)/shard_map/ppermute | solution.py:268
  136.3 50.1 %copy-start.18 = (bf16[256,1280]{1,0:T(8,128)(2,1)S(1)}, bf16[256,1280]{1,0:T(8,128)(2,1)}, u32[]{:S(2)}) copy-start(bf16[256,1280]{1,0:T(8,128)(2,1)} %tokens.3) | copy-start | bytes 1966084
  136.3 50.1 %copy-start.20 = (bf16[256,1280]{1,0:T(8,128)(2,1)S(1)}, bf16[256,1280]{1,0:T(8,128)(2,1)}, u32[]{:S(2)}) copy-start(bf16[256,1280]{1,0:T(8,128)(2,1)} %cotangent.3) | copy-start | bytes 1966084
  136.3 5.6 %collective-permute-start.16 = (bf16[1,96,1280]{2,1,0:T(8,128)(2,1)S(1)}, bf16[1,96,1280]{2,1,0:T(8,128)(2,1)S(1)}, u32[]{:S(2)}, u32[]{:S(2)}) collective-permute-start(bf16[1,96,1280]{2,1,0:T(8,128)(2,1)S(1)} %get-tuple-element.61), channel_id=1, source_target_pairs={{0,32},{32,0},{64,96},{96,64},{128,160},{160,128},{192,224},{224,1... | collective-permute-start | bytes 737288 | tf_op jit(solution)/shard_map/ppermute | solution.py:268
  136.4 5.5 %collective-permute-start.17 = (bf16[1,64,1280]{2,1,0:T(8,128)(2,1)S(1)}, bf16[1,64,1280]{2,1,0:T(8,128)(2,1)S(1)}, u32[]{:S(2)}, u32[]{:S(2)}) collective-permute-start(bf16[1,64,1280]{2,1,0:T(8,128)(2,1)S(1)} %get-tuple-element.65), channel_id=1, source_target_pairs={{0,96},{32,64},{64,32},{96,0},{128,224},{160,192},{192,160},{224,1... | collective-permute-start | bytes 491528 | tf_op jit(solution)/shard_map/ppermute | solution.py:268
  189.8 18.6 %all-to-all-start.2 = ((bf16[32,40,128]{2,1,0:T(8,128)(2,1)}), bf16[32,40,128]{2,1,0:T(8,128)(2,1)}, u32[]{:S(2)}, u32[]{:S(2)}) async-start(bf16[32,40,128]{2,1,0:T(8,128)(2,1)} %bitcast.42), calls=%async_computation.2 | async-start | bytes 655360 | tf_op jit(solution)/shard_map/all_to_all | solution.py:200
  210.1 11.5 %all-to-all-start.3 = ((bf16[8,40,128]{2,1,0:T(8,128)(2,1)}), bf16[8,40,128]{2,1,0:T(8,128)(2,1)}, u32[]{:S(2)}, u32[]{:S(2)}) async-start(bf16[8,40,128]{2,1,0:T(8,128)(2,1)} %broadcast_in_dim.24), calls=%async_computation.3 | async-start | bytes 163840 | tf_op jit(solution)/shard_map/all_to_all | solution.py:200
  219.3 11.4 %copy-start.11 = (bf16[1280,384]{1,0:T(8,128)(2,1)S(1)}, bf16[1280,384]{1,0:T(8,128)(2,1)}, u32[]{:S(2)}) copy-start(bf16[1280,384]{1,0:T(8,128)(2,1)} %copy-done.10) | copy-start | bytes 2949124
  223.2 16.9 %all-to-all-start.4 = ((bf16[32,40,128]{2,1,0:T(8,128)(2,1)}), bf16[32,40,128]{2,1,0:T(8,128)(2,1)S(1)}, u32[]{:S(2)}, u32[]{:S(2)}) async-start(bf16[32,40,128]{2,1,0:T(8,128)(2,1)} %broadcast_in_dim.25), calls=%async_computation.4 | async-start | bytes 655360 | tf_op jit(solution)/shard_map/all_to_all | solution.py:200
  (40 other events, 62.2 us)

commit v2 on v1

v2 whole, which is shorter than its diff:
```python
import functools
import math

import jax
import jax.numpy as jnp
from jax import lax
from jax.experimental import pallas as pl
from jax.experimental.pallas import tpu as pltpu
from jax.sharding import Mesh
from jax.sharding import PartitionSpec as P

F32 = jnp.float32
BF16 = jnp.bfloat16
ALL = ("xl", "yh", "yl", "z", "xh", "c")
DP = ("xl", "yh", "yl")
EXPERT = ("z", "xh", "c")
PLANE = ("xl", "yh", "yl", "xh", "c")

SECTION = 32
PART = 2 * SECTION
HALF = 2 * PART


def neighbour(dim):
    pairs = []
    for i in range(8):
        x, y = divmod(i, 4)
        if dim == "x":
            x = 1 - x
        elif dim == "y1":
            y = y ^ 1
        else:
            y = 3 - y
        pairs.append((i, x * 4 + y))
    return pairs


def call(kernel, out_shape, args, flops, name, scratch=(), memory=pltpu.VMEM, aliases=None):
    shapes = out_shape if isinstance(out_shape, tuple) else (out_shape,)
    moved = sum(math.prod(a.shape) * a.dtype.itemsize for a in tuple(args) + shapes)
    vmem = pl.BlockSpec(memory_space=memory)
    smem = pl.BlockSpec(memory_space=pltpu.SMEM)
    return pl.pallas_call(
        kernel,
        out_shape=out_shape,
        in_specs=[smem if a.dtype == jnp.int32 else vmem for a in args],
        out_specs=(vmem,) * len(shapes) if isinstance(out_shape, tuple) else vmem,
        compiler_params=pltpu.CompilerParams(vmem_limit_bytes=24 * 1024 * 1024),
        scratch_shapes=scratch,
        input_output_aliases=aliases or {},
        cost_estimate=pl.CostEstimate(flops=flops, bytes_accessed=moved, transcendentals=0),
        name=name,
    )(*args)


def dot(a, b, over):
    return lax.dot_general(a, b, (over, ((), ())), preferred_element_type=F32)


PLAIN = ((1,), (0,))
WIDTH = ((1,), (1,))
FIRST = ((0,), (0,))


def spread(slots, wide):
    row = lax.broadcasted_iota(jnp.int32, (slots, wide), 0)
    col = lax.broadcasted_iota(jnp.int32, (slots, wide), 1)
    return (row == 4 * (col // 8) + col % 4).astype(BF16)


def input_columns(shape):
    return lax.broadcasted_iota(jnp.int32, shape, 1) % 8 < 4


LANES = 128


def piece_copies(weights, at_expert, targets, sems, outward):
    copies = []
    target, at = targets[0], 0
    for matrix in weights:
        _, rows, columns = matrix.shape
        for lane in range(0, columns, LANES):
            if at == target.shape[0]:
                target, at = targets[1], 0
            ends = (matrix.at[at_expert, :, pl.ds(lane, LANES)], target.at[pl.ds(at, rows), :])
            source, place = ends if outward else ends[::-1]
            copies.append(pltpu.make_async_copy(source, place, sems.at[len(copies)]))
            at += rows
    for copy in copies:
        copy.start()
    for copy in copies:
        copy.wait()


def pack_kernel(side, expert_in, expert_out, first, second, sems):
    piece_copies((expert_in, expert_out), 1 - side[0], (first, second), sems, True)


def merge_kernel(side, first, second, kept_in, kept_out, grad_in, grad_out, sems):
    piece_copies((grad_in, grad_out), 1 - side[0], (first, second), sems, False)


def unpacked(first, second, width, hidden_units):
    held = first[...]
    cut = width * (hidden_units // LANES)
    w_in = [held[i : i + width] for i in range(0, cut, width)]
    w_out = [held[i : i + hidden_units] for i in range(cut, held.shape[0], hidden_units)]
    held = second[...]
    w_out += [held[i : i + hidden_units] for i in range(0, held.shape[0], hidden_units)]
    return jnp.concatenate(w_in, axis=1), jnp.concatenate(w_out, axis=1)


def prologue_kernel(tokens, router, cotangent, rows, dispatch_out, combine_out):
    slots = router.shape[1]
    wide = 2 * slots
    router_wide = dot(router[...], spread(slots, wide), PLAIN).astype(BF16)
    logits = dot(tokens[...], router_wide, PLAIN)
    down = jnp.exp(logits - jnp.max(logits, axis=0, keepdims=True))
    dispatch = down / jnp.sum(down, axis=0, keepdims=True)
    across = jnp.exp(logits - jnp.max(logits, axis=1, keepdims=True))
    combine = across / (0.5 * jnp.sum(across, axis=1, keepdims=True))
    inputs = input_columns(logits.shape)
    dispatch_b = jnp.where(inputs, dispatch, 0.0).astype(BF16)
    combine_b = jnp.where(inputs, 0.0, combine).astype(BF16)
    total = dot(dispatch_b, tokens[...], FIRST) + dot(combine_b, cotangent[...], FIRST)
    rows[...] = total.astype(BF16)
    dispatch_out[...] = dispatch
    combine_out[...] = combine


def sorting(side, wide):
    q = lax.broadcasted_iota(jnp.int32, (wide, wide), 0)
    r = lax.broadcasted_iota(jnp.int32, (wide, wide), 1)
    expert = (side + q // HALF) % 2
    image = 16 * ((q // PART) % 2) + (q % SECTION) // 2
    kind = (q // SECTION) % 2
    return (r == 8 * image + 4 * kind + 2 * expert + q % 2).astype(BF16)


def sort_kernel(side, rows, keep_a, keep_b, give):
    moved = dot(sorting(side[0], rows.shape[0]), rows[...], PLAIN).astype(BF16)
    keep_a[...] = moved[:PART]
    keep_b[...] = moved[PART:HALF]
    give[...] = moved[HALF:]


def add(a, b):
    return (a.astype(F32) + b.astype(F32)).astype(BF16)


def unsort_kernel(side, a, arrived_a, b, arrived_b, other, out):
    kept = [add(a[...], arrived_a[...]), add(b[...], arrived_b[...]), other[...]]
    rows = jnp.concatenate(kept, axis=0)
    out[...] = dot(sorting(side[0], rows.shape[0]), rows, FIRST).astype(BF16)


def gelu_parts(v):
    cdf = 0.5 * (1.0 + lax.erf(v * math.sqrt(0.5)))
    slope = cdf + v * (jnp.exp(-0.5 * v * v) * (1.0 / math.sqrt(2.0 * math.pi)))
    return v * cdf, slope


def rows_of(blocks, kind):
    first = kind * SECTION
    return jnp.concatenate(
        [
            b[:, first : first + SECTION, :].reshape(b.shape[0] * SECTION, b.shape[2])
            for b in blocks
        ],
        axis=0,
    )


def put_rows(blocks, kind, value):
    at = 0
    first = kind * SECTION
    for b in blocks:
        count = b.shape[0] * SECTION
        part = value[at : at + count].reshape(b.shape[0], SECTION, b.shape[2])
        b[:, first : first + SECTION, :] = part
        at += count


def expert_kernel(side, *refs):
    blocks, (in_all, out_all, first, second) = refs[:4], refs[4:8]
    results, act_out, hid_out = refs[8:12], refs[12], refs[13]
    in_more, out_more = unpacked(first, second, in_all.shape[1], in_all.shape[2])
    kept = side[0]
    rows, grads = rows_of(blocks, 0), rows_of(blocks, 1)
    slot_part = grad_part = 0.0
    for group in range(2):
        w_in = in_all[kept] if group == 0 else in_more
        w_out = out_all[kept] if group == 0 else out_more
        value, slope = gelu_parts(dot(rows, w_in, PLAIN))
        activated = value.astype(BF16)
        grad_hidden = (slope * dot(grads, w_out, WIDTH)).astype(BF16)
        act_out[group] = activated
        hid_out[group] = grad_hidden
        slot_part = slot_part + dot(activated, w_out, PLAIN)
        grad_part = grad_part + dot(grad_hidden, w_in, WIDTH)
    put_rows(results, 0, slot_part.astype(BF16))
    put_rows(results, 1, grad_part.astype(BF16))


def weight_gradients(group, refs):
    blocks, (act_0, act_1, hid_0, hid_1) = refs[:8], refs[8:12]
    rows, grads = rows_of(blocks, 0), rows_of(blocks, 1)
    hidden = jnp.concatenate([hid_0[group], hid_1[group]], axis=0)
    activated = jnp.concatenate([act_0[group], act_1[group]], axis=0)
    grad_in = dot(rows, hidden, FIRST).astype(BF16)
    return grad_in, dot(activated, grads, FIRST).astype(BF16)


def kept_weight_kernel(side, *refs):
    grad_in, grad_out = refs[12:]
    grad_in[side[0]], grad_out[side[0]] = weight_gradients(0, refs)


def given_weight_kernel(*refs):
    targets = refs[12:]
    target, at = targets[0], 0
    for value in weight_gradients(1, refs):
        rows, columns = value.shape
        for lane in range(0, columns, LANES):
            if at == target.shape[0]:
                target, at = targets[1], 0
            target[at : at + rows, :] = value[:, lane : lane + LANES]
            at += rows


def share_kernel(partials, out):
    total = jnp.sum(partials[...].astype(F32), axis=0).astype(BF16)
    for i in range(out.shape[0]):
        out[i] = total


def router_kernel(tokens, cotangent, rows, dispatch_in, combine_in, term, grad_logits_out):
    slots = grad_logits_out.shape[1]
    wide = 2 * slots
    dispatch, combine = dispatch_in[...], combine_in[...]
    inputs = input_columns(dispatch.shape)
    grad_combine = jnp.where(inputs, dot(cotangent[...], rows[...], WIDTH), 0.0)
    grad_dispatch = dot(tokens[...], rows[...], WIDTH)
    logit_combine = combine * (
        grad_combine - jnp.sum(combine * grad_combine, axis=1, keepdims=True)
    )
    logit_dispatch = dispatch * (
        grad_dispatch - jnp.sum(dispatch * grad_dispatch, axis=0, keepdims=True)
    )
    both = logit_combine + pltpu.roll(logit_dispatch, wide - 4, 1)
    both = jnp.where(inputs, both, 0.0).astype(BF16)
    grad_logits = dot(both, spread(slots, wide), WIDTH).astype(BF16)
    grad_logits_out[...] = grad_logits
    term[...] = dot(tokens[...], grad_logits, FIRST).astype(BF16)


def tokens_kernel(rows, router, dispatch_in, combine_in, grad_logits, mixed, grad_tokens):
    inputs = input_columns(dispatch_in.shape)
    combine_b = jnp.where(inputs, combine_in[...], 0.0).astype(BF16)
    dispatch_b = jnp.where(inputs, 0.0, dispatch_in[...]).astype(BF16)
    mixed[...] = dot(combine_b, rows[...], PLAIN).astype(BF16)
    through = dot(dispatch_b, rows[...], PLAIN) + dot(grad_logits[...], router[...], WIDTH)
    grad_tokens[...] = through.astype(BF16)


def shape(dims, dtype=BF16):
    return jax.ShapeDtypeStruct(dims, dtype)


def swap(value, axis):
    return lax.all_to_all(value, axis, split_axis=0, concat_axis=0, tiled=True)


def sum_router(term):
    slots = term.shape[1]
    n_plane = lax.axis_size(PLANE)
    n_z = lax.axis_size("z")
    block = (term.shape[0] // n_plane, slots)
    share = swap(term.reshape((n_plane,) + block), PLANE)
    share = call(share_kernel, shape((n_z,) + block), (share,), 0, "share_plane")
    share = swap(share, "z")
    share = call(share_kernel, shape((n_plane,) + block), (share,), 0, "share_z")
    return swap(share, PLANE).reshape(term.shape).astype(F32)


def per_device(tokens, router, expert_in, expert_out, cotangent):
    n_expert = lax.axis_size(EXPERT)
    count, width = tokens.shape
    slots = router.shape[1]
    wide = 2 * slots
    hidden_units = expert_in.shape[2]
    tied = lax.optimization_barrier
    row, pair = lax.axis_index("yl"), lax.axis_index("yh")
    place = (row + pair) % 2
    side = place.astype(jnp.int32).reshape(1)

    def exchange(value, dim):
        return lax.ppermute(value, DP, neighbour(dim))

    pieces = hidden_units // LANES + width // LANES
    pieces = hidden_units // LANES + width // LANES
    whole = 2 * width * hidden_units // LANES

    def cut(in_pieces, out_pieces):
        first = in_pieces * width + out_pieces * hidden_units
        return shape((first, LANES)), shape((whole - first, LANES))

    copy_sems = (pltpu.SemaphoreType.DMA((pieces,)),)
    packed, packed_late = call(
        pack_kernel,
        cut(3, 3),
        (side, expert_in, expert_out),
        0,
        "pack",
        copy_sems,
        pl.ANY,
    )
    packed, router = tied((packed, router))
    more = exchange(packed, "y1")

    rows, dispatch, combine = call(
        prologue_kernel,
        (shape((wide, width)), shape((count, wide), F32), shape((count, wide), F32)),
        (tokens, router, cotangent),
        6 * count * wide * width,
        "prologue",
    )
    rows = swap(rows.reshape(n_expert, 8, width), EXPERT).reshape(wide, width)
    rows, more = tied((rows, more))
    keep_a, keep_b, give = call(
        sort_kernel,
        (shape((PART, width)), shape((PART, width)), shape((HALF, width))),
        (side, rows),
        2 * wide * wide * width,
        "sort",
    )

    def gather(a, b):
        a, b = a[None], b[None]
        near_a = jnp.concatenate([a, exchange(a, "x")], axis=0)
        near_b = jnp.concatenate([b, exchange(b, "y3")], axis=0)
        near_a, near_b = tied((near_a, near_b))
        return near_a, near_b, exchange(near_a, "y3"), exchange(near_b, "x")

    def experts(blocks, name):
        kept = shape((2, 4 * PART, hidden_units))
        done = call(
            expert_kernel,
            tuple(shape(b.shape) for b in blocks) + (kept, kept),
            (side, *blocks, expert_in, expert_out, more, more_late),
            16 * 4 * PART * width * hidden_units,
            name,
        )
        return done[:4], done[4], done[5]

    taken = exchange(give, "y1")
    packed_late, taken = tied((packed_late, taken))
    more_late = exchange(packed_late, "y1")
    own = gather(keep_a, keep_b)
    partner = gather(taken[:PART], taken[PART:])
    own_done, own_act, own_hid = experts(own, "experts_own")
    far_a, far_b, own_done = tied((partner[2], partner[3], own_done))
    partner = (partner[0], partner[1], far_a, far_b)
    partner_done, partner_act, partner_hid = experts(partner, "experts_partner")

    known = (*own, *partner, own_act, partner_act, own_hid, partner_hid)
    work = 4 * 8 * PART * width * hidden_units
    theirs = call(given_weight_kernel, cut(2, 0), known, work, "weights_given")
    mine = call(
        kept_weight_kernel,
        (shape(expert_in.shape), shape(expert_out.shape)),
        (side, *known),
        work,
        "weights_kept",
    )

    def scatter(done, also):
        near_a, near_b, far_a, far_b = done
        near_a = add(near_a, exchange(far_a, "y3"))
        near_b = add(near_b, exchange(far_b, "x"))
        near_a, near_b, also = tied((near_a, near_b, also))
        arrived_a, arrived_b = exchange(near_a[1], "x"), exchange(near_b[1], "y3")
        return (near_a[0], arrived_a, near_b[0], arrived_b), also

    received = exchange(theirs[0], "y1")
    partner_sum, mine = scatter(partner_done, mine)
    own_sum, _ = scatter(own_done, ())
    a, arrived_a, b, arrived_b = partner_sum
    ready = jnp.concatenate([add(a, arrived_a), add(b, arrived_b)], axis=0)
    ready, received = tied((ready, received))
    returned = exchange(ready, "y1")
    back = call(
        unsort_kernel,
        shape((wide, width)),
        (side, *own_sum, returned),
        2 * wide * wide * width,
        "unsort",
    )
    back, leaving = tied((back, theirs[1]))
    received_late = exchange(leaving, "y1")
    back = swap(back.reshape(n_expert, 8, width), EXPERT).reshape(wide, width)
    term, grad_logits = call(
        router_kernel,
        (shape((width, slots)), shape((count, slots))),
        (tokens, cotangent, back, dispatch, combine),
        6 * count * wide * width,
        "router_gradient",
    )
    mixed, grad_tokens = call(
        tokens_kernel,
        (shape((count, width)), shape((count, width))),
        (back, router, dispatch, combine, grad_logits),
        5 * count * wide * width,
        "token_outputs",
    )
    grad_router = sum_router(term)
    grad_in, grad_out = call(
        merge_kernel,
        (shape(expert_in.shape), shape(expert_out.shape)),
        (side, received, received_late, *mine),
        0,
        "merge",
        copy_sems,
        pl.ANY,
        {3: 0, 4: 1},
    )
    return (mixed, grad_tokens, grad_router, grad_in, grad_out)


def solution(mesh):
    grid = Mesh(mesh.devices.reshape(2, 2, 2, 8, 2, 2), ALL)
    in_specs = (
        P(ALL, None),
        P(),
        P(EXPERT, None, DP),
        P(EXPERT, DP, None),
        P(ALL, None),
    )
    out_specs = (
        P(ALL, None),
        P(ALL, None),
        P(),
        P(EXPERT, None, DP),
        P(EXPERT, DP, None),
    )
    return jax.shard_map(
        per_device, mesh=grid, in_specs=in_specs, out_specs=out_specs, check_vma=False
    )
```

time: 242 us -> 185 us (0.76)
  blocking collectives: 76.4 us -> 57.7 us
  waiting for transfers between devices: 70 us -> 53.9 us
  local copies, waits for them, and re-layouts: 18.3 us -> 6.48 us
  other arithmetic: 9.97 us -> 2.4 us
  starting transfers between devices: 48.1 us -> 44.2 us
    ppermute x18 -> x22, waiting for transfers between devices: 63.3 us -> 27.8 us  [exchange(): return lax.ppermute(value, DP, neighbour(dim))]
    all_to_all x3 -> x2, waiting for transfers between devices: 6.74 us -> 26.1 us  [swap(): return lax.all_to_all(value, axis, split_axis=0, concat_axis=0, tiled=True)]
    all_to_all x2 -> x3, blocking collectives: 76.4 us -> 57.7 us  [swap(): return lax.all_to_all(value, axis, split_axis=0, concat_axis=0, tiled=True)]
    unnamed x102 -> x20, local copies, waits for them, and re-layouts: 16.7 us -> 6.38 us
    another operation x2 -> x0, other arithmetic: 5.84 us -> none  [the longest x1 3.05 us: per_device(): grad_out = jnp.stack([weights(0, 'out'), weights(1, 'out')])]
    ppermute x18 -> x22, starting transfers between devices: 27.3 us -> 22.9 us  [exchange(): return lax.ppermute(value, DP, neighbour(dim))]
    pallas_call x15 -> x13, Pallas kernels: 17 us -> 18.8 us  [call(): pl.pallas_call(kernel, out_shape=out_shape, in_specs=[smem if a.dtype ==...]
    all_to_all x3 -> x2, starting transfers between devices: 20.8 us -> 21.2 us  [swap(): return lax.all_to_all(value, axis, split_axis=0, concat_axis=0, tiled=True)]
  transfers between devices with their start and end apart: 21 -> 24, of which waited for: 16 -> 11; matrix products, arithmetic and copies ran while one was open for 3% -> 0% of each run, Pallas kernels for 6% -> 9%
where the time goes in v2:
time: 185 us; the launch traced here: 184 us
  blocking collectives  57.7 us (31%)
  waiting for transfers between devices  53.9 us (29%)
  starting transfers between devices  44.2 us (24%)
  Pallas kernels  18.8 us (10%)
  local copies, waits for them, and re-layouts  6.48 us (4%)
  other arithmetic  2.4 us (1%)
    all_to_all x3, blocking collectives, swap(): return lax.all_to_all(value, axis, split_axis=0, concat_axis=0, tiled=True)  57.7 us
    ppermute x22, waiting for transfers between devices, exchange(): return lax.ppermute(value, DP, neighbour(dim))  27.8 us
    all_to_all x2, waiting for transfers between devices, swap(): return lax.all_to_all(value, axis, split_axis=0, concat_axis=0, tiled=True)  26.1 us
    ppermute x22, starting transfers between devices, exchange(): return lax.ppermute(value, DP, neighbour(dim))  22.9 us
    all_to_all x2, starting transfers between devices, swap(): return lax.all_to_all(value, axis, split_axis=0, concat_axis=0, tiled=True)  21.2 us
    pallas_call x13, Pallas kernels, call(): pl.pallas_call(kernel, out_shape=out_shape, in_specs=[smem if a.dtype ==...  18.8 us
    unnamed x20, local copies, waits for them, and re-layouts  6.38 us
  transfers between devices with their start and end apart: 24, of which 11 were waited for; matrix products, arithmetic and copies ran while one was open for 0% of the time, Pallas kernels for 9%

profile of v2, /device:TPU:1, one launch (start us, length us, event | category | flops | bytes accessed | tf_op | source)
XLA Modules:
  0.0 184.4 jit_solution(15939013226771471374)
XLA Ops:
  0.7 1.5 copy-done
  2.2 1.5 copy-done.2
  4.2 2.2 %collective-permute-start = (bf16[4992,128]{1,0:T(8,128)(2,1)S(1)}, bf16[4992,128]{1,0:T(8,128)(2,1)S(1)}, u32[]{:S(2)}, u32[]{:S(2)}) collective-permute-start(bf16[4992,128]{1,0:T(8,128)(2,1)S(1)} %get-tuple-element.65), channel_id=1, source_target_pairs={{0,32},{32,0},{64,96},{96,64},{128,160},{160,128},{192,224},{224,1... | collective-permute-start | bytes 3833864 | tf_op jit(solution)/shard_map/ppermute | solution.py:299
  6.5 1.4 prologue.1
  7.9 31.7 %all_to_all.25 = bf16[32,8,1280]{2,1,0:T(8,128)(2,1)S(1)} all-to-all(bf16[32,8,1280]{2,1,0:T(8,128)(2,1)S(1)} %bitcast.36), channel_id=1, replica_groups=mesh['xl'=2,'yh'=2,'yl'=2,'z'=8,'xh'=2,'c'=2] {'z','xh','c'}, dimensions={0} | all-to-all | bytes 1310720 | tf_op jit(solution)/shard_map/all_to_all | solution.py:272
  41.0 2.4 %collective-permute-start.7 = (bf16[1,64,1280]{2,1,0:T(8,128)(2,1)S(1)}, bf16[1,64,1280]{2,1,0:T(8,128)(2,1)S(1)}, u32[]{:S(2)}, u32[]{:S(2)}) collective-permute-start(bf16[1,64,1280]{2,1,0:T(8,128)(2,1)S(1)} %bitcast.38), channel_id=1, source_target_pairs={{0,96},{32,64},{64,32},{96,0},{128,224},{160,192},{192,160},{224,1... | collective-permute-start | bytes 491528 | tf_op jit(solution)/shard_map/ppermute | solution.py:299
  43.4 1.4 collective-permute-done.6
  44.8 3.5 %collective-permute-done.1 = bf16[128,1280]{1,0:T(8,128)(2,1)S(1)} collective-permute-done((bf16[128,1280]{1,0:T(8,128)(2,1)S(1)}, bf16[128,1280]{1,0:T(8,128)(2,1)S(1)}, u32[]{:S(2)}, u32[]{:S(2)}) %collective-permute-start.1) | collective-permute-done | bytes 327712 | tf_op jit(solution)/shard_map/ppermute | solution.py:299
  50.1 2.5 %collective-permute-start.8 = (bf16[2,64,1280]{2,1,0:T(8,128)(2,1)S(1)}, bf16[2,64,1280]{2,1,0:T(8,128)(2,1)S(1)}, u32[]{:S(2)}, u32[]{:S(2)}) collective-permute-start(bf16[2,64,1280]{2,1,0:T(8,128)(2,1)S(1)} %pad_maximum_fusion.2.refs_0_), channel_id=1, source_target_pairs={{0,96},{32,64},{64,32},{96,0},{128,224},{160,192},{192,160},{224,1... | collective-permute-start | bytes 983048 | tf_op jit(solution)/shard_map/ppermute | solution.py:299
  53.3 8.1 %collective-permute-done.3 = bf16[1,64,1280]{2,1,0:T(8,128)(2,1)S(1)} collective-permute-done((bf16[1,64,1280]{2,1,0:T(8,128)(2,1)S(1)}, bf16[1,64,1280]{2,1,0:T(8,128)(2,1)S(1)}, u32[]{:S(2)}, u32[]{:S(2)}) %collective-permute-start.3) | collective-permute-done | bytes 163872 | tf_op jit(solution)/shard_map/ppermute | solution.py:299
  61.4 2.5 %collective-permute-start.4 = (bf16[2,64,1280]{2,1,0:T(8,128)(2,1)S(1)}, bf16[2,64,1280]{2,1,0:T(8,128)(2,1)S(1)}, u32[]{:S(2)}, u32[]{:S(2)}) collective-permute-start(bf16[2,64,1280]{2,1,0:T(8,128)(2,1)S(1)} %pad_maximum_fusion.refs_0_.refs_4_), channel_id=1, source_target_pairs={{0,96},{32,64},{64,32},{96,0},{128,224},{160,192},{192,160},{224,1... | collective-permute-start | bytes 983048 | tf_op jit(solution)/shard_map/ppermute | solution.py:299
  64.2 2.9 %experts_own.1 = (bf16[2,64,1280]{2,1,0:T(8,128)(2,1)S(1)}, bf16[2,64,1280]{2,1,0:T(8,128)(2,1)S(1)}, bf16[2,64,1280]{2,1,0:T(8,128)(2,1)S(1)}, bf16[2,64,1280]{...) custom-call(s32[1]{0:T(128)} %bitcast.side, ...), custom_call_target="tpu_custom_call" | custom-call | flops 2013265920 | bytes 9306116 | tf_op jit(solution)/shard_map/experts_own/pallas_call | solution.py:43
  67.2 1.5 collective-permute-done.4.refs_2_.refs_6_
  68.6 1.5 collective-permute-done.5.refs_3_.refs_7_
  71.3 2.9 %experts_partner.1 = (bf16[2,64,1280]{2,1,0:T(8,128)(2,1)S(1)}, bf16[2,64,1280]{2,1,0:T(8,128)(2,1)S(1)}, bf16[2,64,1280]{2,1,0:T(8,128)(2,1)S(1)}, bf16[2,64,12...) custom-call(s32[1]{0:T(128)} %bitcast.side, ...), custom_call_target="tpu_custom_call" | custom-call | flops 2013265920 | bytes 9306116 | tf_op jit(solution)/shard_map/experts_partner/pallas_call | solution.py:43
  74.3 1.8 %collective-permute-start.15 = (bf16[2,64,1280]{2,1,0:T(8,128)(2,1)S(1)}, bf16[2,64,1280]{2,1,0:T(8,128)(2,1)S(1)}, u32[]{:S(2)}, u32[]{:S(2)}) collective-permute-start(bf16[2,64,1280]{2,1,0:T(8,128)(2,1)S(1)} %get-tuple-element.90), channel_id=1, source_target_pairs={{0,96},{32,64},{64,32},{96,0},{128,224},{160,192},{192,160},{224,1... | collective-permute-start | bytes 983048 | tf_op jit(solution)/shard_map/ppermute | solution.py:299
  77.3 1.4 weights_given.1
  79.8 3.0 %weights_kept.1 = (bf16[2,1280,384]{2,1,0:T(8,128)(2,1)}, bf16[2,384,1280]{2,1,0:T(8,128)(2,1)}) custom-call(s32[1]{0:T(128)} %bitcast.side, bf16[2,64,1280]{2,1,0:T(8,128)(2,1)S(1)} %pad_maximum_fusion.2.refs_0_, bf16[2,64,1280]{2,1,0:T(8,128)(2,1)S(1)} %pad_maximum_fusion.3.refs_1_, bf16[2,64,1280]{2,1,0:T(8,128)(2,1)S(1)} %collective-permute-done.8.refs_2_, ...), custom_call_target="tpu_custom_call" | custom-call | flops 1006632960 | bytes 8126468 | tf_op jit(solution)/shard_map/weights_kept/pallas_call | solution.py:43
  84.9 1.7 collective-permute-start.18
  86.6 2.0 %collective-permute-start.17 = (bf16[64,1280]{1,0:T(8,128)(2,1)S(1)}, bf16[64,1280]{1,0:T(8,128)(2,1)S(1)}, u32[]{:S(2)}, u32[]{:S(2)}) collective-permute-start(bf16[64,1280]{1,0:T(8,128)(2,1)S(1)} %slice_bitcast_fusion.1), channel_id=1, source_target_pairs={{0,128},{32,160},{64,192},{96,224},{128,0},{160,32},{192,64},{224,... | collective-permute-start | bytes 491528 | tf_op jit(solution)/shard_map/ppermute | solution.py:299
  88.6 1.8 collective-permute-done.18
  90.4 2.5 %collective-permute-done.17 = bf16[64,1280]{1,0:T(8,128)(2,1)S(1)} collective-permute-done((bf16[64,1280]{1,0:T(8,128)(2,1)S(1)}, bf16[64,1280]{1,0:T(8,128)(2,1)S(1)}, u32[]{:S(2)}, u32[]{:S(2)}) %collective-permute-start.17) | collective-permute-done | bytes 163872 | tf_op jit(solution)/shard_map/ppermute | solution.py:299
  94.1 6.3 %collective-permute-done.14.arrived_b = bf16[64,1280]{1,0:T(8,128)(2,1)S(1)} collective-permute-done((bf16[64,1280]{1,0:T(8,128)(2,1)S(1)}, bf16[64,1280]{1,0:T(8,128)(2,1)S(1)}, u32[]{:S(2)}, u32[]{:S(2)}) %collective-permute-start.14) | collective-permute-done | bytes 163872 | tf_op jit(solution)/shard_map/ppermute | solution.py:299
  101.8 13.5 %all-to-all-start.1 = ((bf16[32,8,1280]{2,1,0:T(8,128)(2,1)}), bf16[32,8,1280]{2,1,0:T(8,128)(2,1)S(1)}, u32[]{:S(2)}, u32[]{:S(2)}) async-start(bf16[32,8,1280]{2,1,0:T(8,128)(2,1)} %bitcast.15), calls=%async_computation.1 | async-start | bytes 1310720 | tf_op jit(solution)/shard_map/all_to_all | solution.py:272
  115.7 19.5 %all-to-all-done.1 = bf16[32,8,1280]{2,1,0:T(8,128)(2,1)S(1)} async-done(((bf16[32,8,1280]{2,1,0:T(8,128)(2,1)}), bf16[32,8,1280]{2,1,0:T(8,128)(2,1)S(1)}, u32[]{:S(2)}, u32[]{:S(2)}) %all-to-all-start.1) | async-done | bytes 655392 | tf_op jit(solution)/shard_map/all_to_all | solution.py:272
  138.5 15.8 %all_to_all.26.partials = bf16[32,40,128]{2,1,0:T(8,128)(2,1)S(1)} all-to-all(bf16[32,40,128]{2,1,0:T(8,128)(2,1)S(1)} %bitcast.37), channel_id=1, replica_groups=mesh['xl'=2,'yh'=2,'yl'=2,'z'=8,'xh'=2,'c'=2] {'xl','yh','yl','xh','c'}, dimensions={0} | all-to-all | bytes 655360 | tf_op jit(solution)/shard_map/all_to_all | solution.py:272
  154.4 10.1 %all_to_all.27.partials = bf16[8,40,128]{2,1,0:T(8,128)(2,1)S(1)} all-to-all(bf16[8,40,128]{2,1,0:T(8,128)(2,1)S(1)} %share_plane.1), channel_id=1, replica_groups=mesh['xl'=2,'yh'=2,'yl'=2,'z'=8,'xh'=2,'c'=2] {'z'}, dimensions={0} | all-to-all | bytes 163840 | tf_op jit(solution)/shard_map/all_to_all | solution.py:272
  165.3 7.8 %all-to-all-start.4 = ((bf16[32,40,128]{2,1,0:T(8,128)(2,1)}), bf16[32,40,128]{2,1,0:T(8,128)(2,1)}, u32[]{:S(2)}, u32[]{:S(2)}) async-start(bf16[32,40,128]{2,1,0:T(8,128)(2,1)} %share_z.1), calls=%async_computation.4 | async-start | bytes 655360 | tf_op jit(solution)/shard_map/all_to_all | solution.py:272
  173.0 1.5 token_outputs.1
  174.6 1.4 merge.1
  175.9 6.6 %all-to-all-done.4 = bf16[32,40,128]{2,1,0:T(8,128)(2,1)} async-done(((bf16[32,40,128]{2,1,0:T(8,128)(2,1)}), bf16[32,40,128]{2,1,0:T(8,128)(2,1)}, u32[]{:S(2)}, u32[]{:S(2)}) %all-to-all-start.4) | async-done | bytes 327712 | tf_op jit(solution)/shard_map/all_to_all | solution.py:272
  182.6 1.9 %bitcast_convert_fusion = f32[1280,128]{1,0:T(8,128)} fusion(bf16[32,40,128]{2,1,0:T(8,128)(2,1)} %all-to-all-done.4), kind=kLoop, calls=%fused_computation.9 | loop fusion | flops 163840 | bytes 983040 | tf_op jit(solution)/shard_map/convert_element_type | solution.py:284
  (69 shorter events, 17.3 us)
Async XLA Ops:
  0.6 1.5 copy-start
  2.2 1.5 copy-start.2
  3.7 2.7 %copy-start.4 = (bf16[256,1280]{1,0:T(8,128)(2,1)S(1)}, bf16[256,1280]{1,0:T(8,128)(2,1)}, u32[]{:S(2)}) copy-start(bf16[256,1280]{1,0:T(8,128)(2,1)} %tokens.3) | copy-start | bytes 1966084
  3.7 2.7 %copy-start.6 = (bf16[256,1280]{1,0:T(8,128)(2,1)S(1)}, bf16[256,1280]{1,0:T(8,128)(2,1)}, u32[]{:S(2)}) copy-start(bf16[256,1280]{1,0:T(8,128)(2,1)} %cotangent.3) | copy-start | bytes 1966084
  3.7 2.7 %copy-start.8 = (bf16[1280,128]{1,0:T(8,128)(2,1)S(1)}, bf16[1280,128]{1,0:T(8,128)(2,1)}, u32[]{:S(2)}) copy-start(bf16[1280,128]{1,0:T(8,128)(2,1)} %router.1) | copy-start | bytes 983044
  4.2 35.4 %collective-permute-start = (bf16[4992,128]{1,0:T(8,128)(2,1)S(1)}, bf16[4992,128]{1,0:T(8,128)(2,1)S(1)}, u32[]{:S(2)}, u32[]{:S(2)}) collective-permute-start(bf16[4992,128]{1,0:T(8,128)(2,1)S(1)} %get-tuple-element.65), channel_id=1, source_target_pairs={{0,32},{32,0},{64,96},{96,64},{128,160},{160,128},{192,224},{224,1... | collective-permute-start | bytes 3833864 | tf_op jit(solution)/shard_map/ppermute | solution.py:299
  39.6 24.6 %copy-start.1 = (bf16[2,1280,384]{2,1,0:T(8,128)(2,1)S(1)}, bf16[2,1280,384]{2,1,0:T(8,128)(2,1)}, u32[]{:S(2)}) copy-start(bf16[2,1280,384]{2,1,0:T(8,128)(2,1)} %refs_4_.3) | copy-start | bytes 5898244
  39.6 24.6 %copy-start.3 = (bf16[2,384,1280]{2,1,0:T(8,128)(2,1)S(1)}, bf16[2,384,1280]{2,1,0:T(8,128)(2,1)}, u32[]{:S(2)}) copy-start(bf16[2,384,1280]{2,1,0:T(8,128)(2,1)} %refs_5_.3) | copy-start | bytes 5898244
  40.1 4.7 %collective-permute-start.6 = (bf16[1,64,1280]{2,1,0:T(8,128)(2,1)S(1)}, bf16[1,64,1280]{2,1,0:T(8,128)(2,1)S(1)}, u32[]{:S(2)}, u32[]{:S(2)}) collective-permute-start(bf16[1,64,1280]{2,1,0:T(8,128)(2,1)S(1)} %bitcast.40), channel_id=1, source_target_pairs={{0,128},{32,160},{64,192},{96,224},{128,0},{160,32},{192,64},{224,... | collective-permute-start | bytes 491528 | tf_op jit(solution)/shard_map/ppermute | solution.py:299
  40.5 7.9 %collective-permute-start.1 = (bf16[128,1280]{1,0:T(8,128)(2,1)S(1)}, bf16[128,1280]{1,0:T(8,128)(2,1)S(1)}, u32[]{:S(2)}, u32[]{:S(2)}) collective-permute-start(bf16[128,1280]{1,0:T(8,128)(2,1)S(1)} %get-tuple-element.67), channel_id=1, source_target_pairs={{0,32},{32,0},{64,96},{96,64},{128,160},{160,128},{192,224},{224,1... | collective-permute-start | bytes 983048 | tf_op jit(solution)/shard_map/ppermute | solution.py:299
  41.0 9.1 %collective-permute-start.7 = (bf16[1,64,1280]{2,1,0:T(8,128)(2,1)S(1)}, bf16[1,64,1280]{2,1,0:T(8,128)(2,1)S(1)}, u32[]{:S(2)}, u32[]{:S(2)}) collective-permute-start(bf16[1,64,1280]{2,1,0:T(8,128)(2,1)S(1)} %bitcast.38), channel_id=1, source_target_pairs={{0,96},{32,64},{64,32},{96,0},{128,224},{160,192},{192,160},{224,1... | collective-permute-start | bytes 491528 | tf_op jit(solution)/shard_map/ppermute | solution.py:299
  48.4 4.9 %collective-permute-start.2 = (bf16[1,64,1280]{2,1,0:T(8,128)(2,1)S(1)}, bf16[1,64,1280]{2,1,0:T(8,128)(2,1)S(1)}, u32[]{:S(2)}, u32[]{:S(2)}) collective-permute-start(bf16[1,64,1280]{2,1,0:T(8,128)(2,1)S(1)} %get-tuple-element.122), channel_id=1, source_target_pairs={{0,128},{32,160},{64,192},{96,224},{128,0},{160,32},{192,64},{224,... | collective-permute-start | bytes 491528 | tf_op jit(solution)/shard_map/ppermute | solution.py:299
  49.6 14.6 %collective-permute-start.10 = (bf16[2688,128]{1,0:T(8,128)(2,1)S(1)}, bf16[2688,128]{1,0:T(8,128)(2,1)S(1)}, u32[]{:S(2)}, u32[]{:S(2)}) collective-permute-start(bf16[2688,128]{1,0:T(8,128)(2,1)S(1)} %get-tuple-element.76), channel_id=1, source_target_pairs={{0,32},{32,0},{64,96},{96,64},{128,160},{160,128},{192,224},{224,1... | collective-permute-start | bytes 2064392 | tf_op jit(solution)/shard_map/ppermute | solution.py:299
  50.1 14.0 %collective-permute-start.8 = (bf16[2,64,1280]{2,1,0:T(8,128)(2,1)S(1)}, bf16[2,64,1280]{2,1,0:T(8,128)(2,1)S(1)}, u32[]{:S(2)}, u32[]{:S(2)}) collective-permute-start(bf16[2,64,1280]{2,1,0:T(8,128)(2,1)S(1)} %pad_maximum_fusion.2.refs_0_), channel_id=1, source_target_pairs={{0,96},{32,64},{64,32},{96,0},{128,224},{160,192},{192,160},{224,1... | collective-permute-start | bytes 983048 | tf_op jit(solution)/shard_map/ppermute | solution.py:299
  52.6 11.5 %collective-permute-start.9 = (bf16[2,64,1280]{2,1,0:T(8,128)(2,1)S(1)}, bf16[2,64,1280]{2,1,0:T(8,128)(2,1)S(1)}, u32[]{:S(2)}, u32[]{:S(2)}) collective-permute-start(bf16[2,64,1280]{2,1,0:T(8,128)(2,1)S(1)} %pad_maximum_fusion.3.refs_1_), channel_id=1, source_target_pairs={{0,128},{32,160},{64,192},{96,224},{128,0},{160,32},{192,64},{224,... | collective-permute-start | bytes 983048 | tf_op jit(solution)/shard_map/ppermute | solution.py:299
  52.9 8.4 %collective-permute-start.3 = (bf16[1,64,1280]{2,1,0:T(8,128)(2,1)S(1)}, bf16[1,64,1280]{2,1,0:T(8,128)(2,1)S(1)}, u32[]{:S(2)}, u32[]{:S(2)}) collective-permute-start(bf16[1,64,1280]{2,1,0:T(8,128)(2,1)S(1)} %get-tuple-element.121), channel_id=1, source_target_pairs={{0,96},{32,64},{64,32},{96,0},{128,224},{160,192},{192,160},{224,1... | collective-permute-start | bytes 491528 | tf_op jit(solution)/shard_map/ppermute | solution.py:299
  61.4 7.2 %collective-permute-start.4 = (bf16[2,64,1280]{2,1,0:T(8,128)(2,1)S(1)}, bf16[2,64,1280]{2,1,0:T(8,128)(2,1)S(1)}, u32[]{:S(2)}, u32[]{:S(2)}) collective-permute-start(bf16[2,64,1280]{2,1,0:T(8,128)(2,1)S(1)} %pad_maximum_fusion.refs_0_.refs_4_), channel_id=1, source_target_pairs={{0,96},{32,64},{64,32},{96,0},{128,224},{160,192},{192,160},{224,1... | collective-permute-start | bytes 983048 | tf_op jit(solution)/shard_map/ppermute | solution.py:299
  63.9 6.2 %collective-permute-start.5 = (bf16[2,64,1280]{2,1,0:T(8,128)(2,1)S(1)}, bf16[2,64,1280]{2,1,0:T(8,128)(2,1)S(1)}, u32[]{:S(2)}, u32[]{:S(2)}) collective-permute-start(bf16[2,64,1280]{2,1,0:T(8,128)(2,1)S(1)} %pad_maximum_fusion.1.refs_1_.refs_5_), channel_id=1, source_target_pairs={{0,128},{32,160},{64,192},{96,224},{128,0},{160,32},{192,64},{224,... | collective-permute-start | bytes 983048 | tf_op jit(solution)/shard_map/ppermute | solution.py:299
  70.1 12.7 %collective-permute-start.11 = (bf16[2,64,1280]{2,1,0:T(8,128)(2,1)S(1)}, bf16[2,64,1280]{2,1,0:T(8,128)(2,1)S(1)}, u32[]{:S(2)}, u32[]{:S(2)}) collective-permute-start(bf16[2,64,1280]{2,1,0:T(8,128)(2,1)S(1)} %get-tuple-element.82), channel_id=1, source_target_pairs={{0,96},{32,64},{64,32},{96,0},{128,224},{160,192},{192,160},{224,1... | collective-permute-start | bytes 983048 | tf_op jit(solution)/shard_map/ppermute | solution.py:299
  71.0 11.9 %collective-permute-start.12 = (bf16[2,64,1280]{2,1,0:T(8,128)(2,1)S(1)}, bf16[2,64,1280]{2,1,0:T(8,128)(2,1)S(1)}, u32[]{:S(2)}, u32[]{:S(2)}) collective-permute-start(bf16[2,64,1280]{2,1,0:T(8,128)(2,1)S(1)} %get-tuple-element.84), channel_id=1, source_target_pairs={{0,128},{32,160},{64,192},{96,224},{128,0},{160,32},{192,64},{224,... | collective-permute-start | bytes 983048 | tf_op jit(solution)/shard_map/ppermute | solution.py:299
  74.3 9.2 %collective-permute-start.15 = (bf16[2,64,1280]{2,1,0:T(8,128)(2,1)S(1)}, bf16[2,64,1280]{2,1,0:T(8,128)(2,1)S(1)}, u32[]{:S(2)}, u32[]{:S(2)}) collective-permute-start(bf16[2,64,1280]{2,1,0:T(8,128)(2,1)S(1)} %get-tuple-element.90), channel_id=1, source_target_pairs={{0,96},{32,64},{64,32},{96,0},{128,224},{160,192},{192,160},{224,1... | collective-permute-start | bytes 983048 | tf_op jit(solution)/shard_map/ppermute | solution.py:299
  76.1 8.7 %collective-permute-start.16 = (bf16[2,64,1280]{2,1,0:T(8,128)(2,1)S(1)}, bf16[2,64,1280]{2,1,0:T(8,128)(2,1)S(1)}, u32[]{:S(2)}, u32[]{:S(2)}) collective-permute-start(bf16[2,64,1280]{2,1,0:T(8,128)(2,1)S(1)} %get-tuple-element.92), channel_id=1, source_target_pairs={{0,128},{32,160},{64,192},{96,224},{128,0},{160,32},{192,64},{224,... | collective-permute-start | bytes 983048 | tf_op jit(solution)/shard_map/ppermute | solution.py:299
  78.7 1.1 copy-start.9
  79.8 13.1 %collective-permute-start.19 = (bf16[2560,128]{1,0:T(8,128)(2,1)S(1)}, bf16[2560,128]{1,0:T(8,128)(2,1)S(1)}, u32[]{:S(2)}, u32[]{:S(2)}) collective-permute-start(bf16[2560,128]{1,0:T(8,128)(2,1)S(1)} %get-tuple-element.101), channel_id=1, source_target_pairs={{0,32},{32,0},{64,96},{96,64},{128,160},{160,128},{192,224},{224,1... | collective-permute-start | bytes 1966088 | tf_op jit(solution)/shard_map/ppermute | solution.py:299
  83.0 11.0 %collective-permute-start.13 = (bf16[64,1280]{1,0:T(8,128)(2,1)S(1)}, bf16[64,1280]{1,0:T(8,128)(2,1)S(1)}, u32[]{:S(2)}, u32[]{:S(2)}) collective-permute-start(bf16[64,1280]{1,0:T(8,128)(2,1)S(1)} %get-tuple-element.119), channel_id=1, source_target_pairs={{0,128},{32,160},{64,192},{96,224},{128,0},{160,32},{192,64},{224,... | collective-permute-start | bytes 491528 | tf_op jit(solution)/shard_map/ppermute | solution.py:299
  84.9 5.5 %collective-permute-start.18 = (bf16[64,1280]{1,0:T(8,128)(2,1)S(1)}, bf16[64,1280]{1,0:T(8,128)(2,1)S(1)}, u32[]{:S(2)}, u32[]{:S(2)}) collective-permute-start(bf16[64,1280]{1,0:T(8,128)(2,1)S(1)} %slice_bitcast_fusion), channel_id=1, source_target_pairs={{0,96},{32,64},{64,32},{96,0},{128,224},{160,192},{192,160},{224,1... | collective-permute-start | bytes 491528 | tf_op jit(solution)/shard_map/ppermute | solution.py:299
  86.6 6.2 %collective-permute-start.17 = (bf16[64,1280]{1,0:T(8,128)(2,1)S(1)}, bf16[64,1280]{1,0:T(8,128)(2,1)S(1)}, u32[]{:S(2)}, u32[]{:S(2)}) collective-permute-start(bf16[64,1280]{1,0:T(8,128)(2,1)S(1)} %slice_bitcast_fusion.1), channel_id=1, source_target_pairs={{0,128},{32,160},{64,192},{96,224},{128,0},{160,32},{192,64},{224,... | collective-permute-start | bytes 491528 | tf_op jit(solution)/shard_map/ppermute | solution.py:299
  92.9 7.5 %collective-permute-start.20 = (bf16[128,1280]{1,0:T(8,128)(2,1)S(1)}, bf16[128,1280]{1,0:T(8,128)(2,1)S(1)}, u32[]{:S(2)}, u32[]{:S(2)}) collective-permute-start(bf16[128,1280]{1,0:T(8,128)(2,1)S(1)} %pad_maximum_fusion.4), channel_id=1, source_target_pairs={{0,32},{32,0},{64,96},{96,64},{128,160},{160,128},{192,224},{224,1... | collective-permute-start | bytes 983048 | tf_op jit(solution)/shard_map/ppermute | solution.py:299
  93.1 7.3 %collective-permute-start.14 = (bf16[64,1280]{1,0:T(8,128)(2,1)S(1)}, bf16[64,1280]{1,0:T(8,128)(2,1)S(1)}, u32[]{:S(2)}, u32[]{:S(2)}) collective-permute-start(bf16[64,1280]{1,0:T(8,128)(2,1)S(1)} %get-tuple-element.117), channel_id=1, source_target_pairs={{0,96},{32,64},{64,32},{96,0},{128,224},{160,192},{192,160},{224,1... | collective-permute-start | bytes 491528 | tf_op jit(solution)/shard_map/ppermute | solution.py:299
  101.8 33.4 %all-to-all-start.1 = ((bf16[32,8,1280]{2,1,0:T(8,128)(2,1)}), bf16[32,8,1280]{2,1,0:T(8,128)(2,1)S(1)}, u32[]{:S(2)}, u32[]{:S(2)}) async-start(bf16[32,8,1280]{2,1,0:T(8,128)(2,1)} %bitcast.15), calls=%async_computation.1 | async-start | bytes 1310720 | tf_op jit(solution)/shard_map/all_to_all | solution.py:272
  115.2 59.3 %collective-permute-start.21 = (bf16[5120,128]{1,0:T(8,128)(2,1)}, bf16[5120,128]{1,0:T(8,128)(2,1)S(1)}, u32[]{:S(2)}, u32[]{:S(2)}) collective-permute-start(bf16[5120,128]{1,0:T(8,128)(2,1)} %copy-done.9), channel_id=1, source_target_pairs={{0,32},{32,0},{64,96},{96,64},{128,160},{160,128},{192,224},{224,1... | collective-permute-start | bytes 3932168 | tf_op jit(solution)/shard_map/ppermute | solution.py:299
  165.3 17.3 %all-to-all-start.4 = ((bf16[32,40,128]{2,1,0:T(8,128)(2,1)}), bf16[32,40,128]{2,1,0:T(8,128)(2,1)}, u32[]{:S(2)}, u32[]{:S(2)}) async-start(bf16[32,40,128]{2,1,0:T(8,128)(2,1)} %share_z.1), calls=%async_computation.4 | async-start | bytes 655360 | tf_op jit(solution)/shard_map/all_to_all | solution.py:272
  (2 other events, 2.2 us)

commit v3 on v2

--- a/solution.py
+++ b/solution.py
@@ -14,7 +14,8 @@
 ALL = ("xl", "yh", "yl", "z", "xh", "c")
 DP = ("xl", "yh", "yl")
 EXPERT = ("z", "xh", "c")
-PLANE = ("xl", "yh", "yl", "xh", "c")
+PLANE = ("xl", "yh", "yl", "xh")
+CORES = [(0, 1), (1, 0)]
 
 SECTION = 32
 PART = 2 * SECTION
@@ -235,7 +236,13 @@
         out[i] = total
 
 
-def router_kernel(tokens, cotangent, rows, dispatch_in, combine_in, term, grad_logits_out):
+def by_core(core, first, second):
+    return jnp.where(core == 0, first, second), jnp.where(core == 0, second, first)
+
+
+def router_kernel(
+    core, tokens, cotangent, rows, dispatch_in, combine_in, keep, give, grad_logits_out
+):
     slots = grad_logits_out.shape[1]
     wide = 2 * slots
     dispatch, combine = dispatch_in[...], combine_in[...]
@@ -252,7 +259,10 @@
     both = jnp.where(inputs, both, 0.0).astype(BF16)
     grad_logits = dot(both, spread(slots, wide), WIDTH).astype(BF16)
     grad_logits_out[...] = grad_logits
-    term[...] = dot(tokens[...], grad_logits, FIRST).astype(BF16)
+    term = dot(tokens[...], grad_logits, FIRST)
+    kept, given = by_core(core[0], term[: keep.shape[0]], term[keep.shape[0] :])
+    keep[...] = kept.astype(BF16)
+    give[...] = given.astype(BF16)
 
 
 def tokens_kernel(rows, router, dispatch_in, combine_in, grad_logits, mixed, grad_tokens):
@@ -264,6 +274,17 @@
     grad_tokens[...] = through.astype(BF16)
 
 
+def pair_kernel(keep, received, out):
+    out[...] = add(keep[...], received[...])
+
+
+def widen_kernel(core, kept, received, out):
+    half = out.shape[0] // 2
+    kept = kept[...].astype(F32).reshape(half, out.shape[1])
+    received = received[...].astype(F32).reshape(half, out.shape[1])
+    out[:half, :], out[half:, :] = by_core(core[0], kept, received)
+
+
 def shape(dims, dtype=BF16):
     return jax.ShapeDtypeStruct(dims, dtype)
 
@@ -272,16 +293,21 @@
     return lax.all_to_all(value, axis, split_axis=0, concat_axis=0, tiled=True)
 
 
-def sum_router(term):
-    slots = term.shape[1]
+def sum_router(keep, give, core, others):
+    half, slots = keep.shape
     n_plane = lax.axis_size(PLANE)
     n_z = lax.axis_size("z")
-    block = (term.shape[0] // n_plane, slots)
-    share = swap(term.reshape((n_plane,) + block), PLANE)
+    block = (half // n_plane, slots)
+    received = lax.ppermute(give, "c", CORES)
+    share = call(pair_kernel, shape(keep.shape), (keep, received), 0, "pair")
+    share = swap(share.reshape((n_plane,) + block), PLANE)
     share = call(share_kernel, shape((n_z,) + block), (share,), 0, "share_plane")
     share = swap(share, "z")
     share = call(share_kernel, shape((n_plane,) + block), (share,), 0, "share_z")
-    return swap(share, PLANE).reshape(term.shape).astype(F32)
+    share, others = lax.optimization_barrier((swap(share, PLANE), others))
+    received = lax.ppermute(share, "c", CORES)
+    full = shape((2 * half, slots), F32)
+    return call(widen_kernel, full, (core, share, received), 0, "widen"), others
 
 
 def per_device(tokens, router, expert_in, expert_out, cotangent):
@@ -294,6 +320,7 @@
     row, pair = lax.axis_index("yl"), lax.axis_index("yh")
     place = (row + pair) % 2
     side = place.astype(jnp.int32).reshape(1)
+    core = lax.axis_index("c").astype(jnp.int32).reshape(1)
 
     def exchange(value, dim):
         return lax.ppermute(value, DP, neighbour(dim))
@@ -336,12 +363,14 @@
         "sort",
     )
 
-    def gather(a, b):
+    def first_step(a, b):
         a, b = a[None], b[None]
         near_a = jnp.concatenate([a, exchange(a, "x")], axis=0)
         near_b = jnp.concatenate([b, exchange(b, "y3")], axis=0)
-        near_a, near_b = tied((near_a, near_b))
-        return near_a, near_b, exchange(near_a, "y3"), exchange(near_b, "x")
+        return tied((near_a, near_b))
+
+    def second_step(a, b):
+        return a, b, exchange(a, "y3"), exchange(b, "x")
 
     def experts(blocks, name):
         kept = shape((2, 4 * PART, hidden_units))
@@ -357,12 +386,14 @@
     taken = exchange(give, "y1")
     packed_late, taken = tied((packed_late, taken))
     more_late = exchange(packed_late, "y1")
-    own = gather(keep_a, keep_b)
-    partner = gather(taken[:PART], taken[PART:])
+    partner = first_step(taken[:PART], taken[PART:])
+    own = first_step(keep_a, keep_b)
+    partner, own = tied((partner, own))
+    partner, own = second_step(*partner), second_step(*own)
+    partner_done, partner_act, partner_hid = experts(partner, "experts_partner")
+    far_a, far_b, partner_done = tied((own[2], own[3], partner_done))
+    own = (own[0], own[1], far_a, far_b)
     own_done, own_act, own_hid = experts(own, "experts_own")
-    far_a, far_b, own_done = tied((partner[2], partner[3], own_done))
-    partner = (partner[0], partner[1], far_a, far_b)
-    partner_done, partner_act, partner_hid = experts(partner, "experts_partner")
 
     known = (*own, *partner, own_act, partner_act, own_hid, partner_hid)
     work = 4 * 8 * PART * width * hidden_units
@@ -375,17 +406,19 @@
         "weights_kept",
     )
 
-    def scatter(done, also):
-        near_a, near_b, far_a, far_b = done
-        near_a = add(near_a, exchange(far_a, "y3"))
-        near_b = add(near_b, exchange(far_b, "x"))
+    def first_sum(near_a, near_b, far_a, far_b):
+        return add(near_a, exchange(far_a, "y3")), add(near_b, exchange(far_b, "x"))
+
+    def second_sum(near_a, near_b, also):
         near_a, near_b, also = tied((near_a, near_b, also))
         arrived_a, arrived_b = exchange(near_a[1], "x"), exchange(near_b[1], "y3")
         return (near_a[0], arrived_a, near_b[0], arrived_b), also
 
     received = exchange(theirs[0], "y1")
-    partner_sum, mine = scatter(partner_done, mine)
-    own_sum, _ = scatter(own_done, ())
+    partner_sum = first_sum(*partner_done)
+    partner_sum, own_done = tied((partner_sum, own_done))
+    partner_sum, _ = second_sum(*partner_sum, ())
+    own_sum, mine = second_sum(*first_sum(*own_done), mine)
     a, arrived_a, b, arrived_b = partner_sum
     ready = jnp.concatenate([add(a, arrived_a), add(b, arrived_b)], axis=0)
     ready, received = tied((ready, received))
@@ -400,10 +433,10 @@
     back, leaving = tied((back, theirs[1]))
     received_late = exchange(leaving, "y1")
     back = swap(back.reshape(n_expert, 8, width), EXPERT).reshape(wide, width)
-    term, grad_logits = call(
+    keep, give, grad_logits = call(
         router_kernel,
-        (shape((width, slots)), shape((count, slots))),
-        (tokens, cotangent, back, dispatch, combine),
+        (shape((width // 2, slots)), shape((width // 2, slots)), shape((count, slots))),
+        (core, tokens, cotangent, back, dispatch, combine),
         6 * count * wide * width,
         "router_gradient",
     )
@@ -414,7 +447,6 @@
         5 * count * wide * width,
         "token_outputs",
     )
-    grad_router = sum_router(term)
     grad_in, grad_out = call(
         merge_kernel,
         (shape(expert_in.shape), shape(expert_out.shape)),
@@ -425,6 +457,10 @@
         pl.ANY,
         {3: 0, 4: 1},
     )
+    grad_router, others = sum_router(
+        keep, give, core, (mixed, grad_tokens, grad_in, grad_out)
+    )
+    mixed, grad_tokens, grad_in, grad_out = others
     return (mixed, grad_tokens, grad_router, grad_in, grad_out)
 
 

time: 185 us -> 181 us (0.978)
  starting transfers between devices: 44.2 us -> 49.7 us
  waiting for transfers between devices: 53.9 us -> 48.4 us
  blocking collectives: 57.7 us -> 53.9 us
  other arithmetic: 2.4 us -> 0.54 us
    ppermute x0 -> x2, starting transfers between devices: none -> 5.49 us  [the longest x1 4.35 us: sum_router(): received = lax.ppermute(share, 'c', CORES)]
    ppermute x22, waiting for transfers between devices: 27.8 us -> 23.7 us  [exchange(): return lax.ppermute(value, DP, neighbour(dim))]
    all_to_all x3, blocking collectives: 57.7 us -> 53.9 us  [swap(): return lax.all_to_all(value, axis, split_axis=0, concat_axis=0, tiled=True)]
    all_to_all x2, waiting for transfers between devices: 26.1 us -> 22.7 us  [swap(): return lax.all_to_all(value, axis, split_axis=0, concat_axis=0, tiled=True)]
    ppermute x0 -> x2, waiting for transfers between devices: none -> 2.06 us  [the longest x1 1.03 us: sum_router(): received = lax.ppermute(give, 'c', CORES)]
    convert_element_type x1 -> x0, other arithmetic: 1.85 us -> none  [sum_router(): return swap(share, PLANE).reshape(term.shape).astype(F32)]
    unnamed x20 -> x22, local copies, waits for them, and re-layouts: 6.38 us -> 7.34 us
    pallas_call x13 -> x15, Pallas kernels: 18.8 us -> 19.7 us  [call(): pl.pallas_call(kernel, out_shape=out_shape, in_specs=[smem if a.dtype ==...]
  transfers between devices with their start and end apart: 24 -> 26, of which waited for: 11 -> 17; matrix products, arithmetic and copies ran while one was open for 0% -> 0% of each run, Pallas kernels for 9% -> 9%
where the time goes in v3:
time: 181 us
  blocking collectives  53.9 us (30%)
  starting transfers between devices  49.7 us (27%)
  waiting for transfers between devices  48.4 us (27%)
  Pallas kernels  19.7 us (11%)
  local copies, waits for them, and re-layouts  7.43 us (4%)
    all_to_all x3, blocking collectives, swap(): return lax.all_to_all(value, axis, split_axis=0, concat_axis=0, tiled=True)  53.9 us
    ppermute x22, waiting for transfers between devices, exchange(): return lax.ppermute(value, DP, neighbour(dim))  23.7 us
    ppermute x22, starting transfers between devices, exchange(): return lax.ppermute(value, DP, neighbour(dim))  23.6 us
    all_to_all x2, waiting for transfers between devices, swap(): return lax.all_to_all(value, axis, split_axis=0, concat_axis=0, tiled=True)  22.7 us
    all_to_all x2, starting transfers between devices, swap(): return lax.all_to_all(value, axis, split_axis=0, concat_axis=0, tiled=True)  20.6 us
    pallas_call x15, Pallas kernels, call(): pl.pallas_call(kernel, out_shape=out_shape, in_specs=[smem if a.dtype ==...  19.7 us
    unnamed x22, local copies, waits for them, and re-layouts  7.34 us
    ppermute x1, starting transfers between devices, sum_router(): received = lax.ppermute(share, 'c', CORES)  4.35 us
  transfers between devices with their start and end apart: 26, of which 17 were waited for; matrix products, arithmetic and copies ran while one was open for 0% of the time, Pallas kernels for 9%

profile of v3, /device:TPU:1, one launch (start us, length us, event | category | flops | bytes accessed | tf_op | source)
XLA Modules:
  0.0 180.6 jit_solution(12957265412244345821)
XLA Ops:
  0.7 1.5 copy-done
  2.2 1.5 copy-done.2
  4.2 2.2 %collective-permute-start = (bf16[4992,128]{1,0:T(8,128)(2,1)S(1)}, bf16[4992,128]{1,0:T(8,128)(2,1)S(1)}, u32[]{:S(2)}, u32[]{:S(2)}) collective-permute-start(bf16[4992,128]{1,0:T(8,128)(2,1)S(1)} %get-tuple-element.81), channel_id=1, source_target_pairs={{0,32},{32,0},{64,96},{96,64},{128,160},{160,128},{192,224},{224,1... | collective-permute-start | bytes 3833864 | tf_op jit(solution)/shard_map/ppermute | solution.py:326
  6.5 1.4 prologue.1
  7.9 31.7 %all_to_all.25 = bf16[32,8,1280]{2,1,0:T(8,128)(2,1)S(1)} all-to-all(bf16[32,8,1280]{2,1,0:T(8,128)(2,1)S(1)} %bitcast.34), channel_id=1, replica_groups=mesh['xl'=2,'yh'=2,'yl'=2,'z'=8,'xh'=2,'c'=2] {'z','xh','c'}, dimensions={0} | all-to-all | bytes 1310720 | tf_op jit(solution)/shard_map/all_to_all | solution.py:293
  41.0 2.4 %collective-permute-start.5 = (bf16[1,64,1280]{2,1,0:T(8,128)(2,1)S(1)}, bf16[1,64,1280]{2,1,0:T(8,128)(2,1)S(1)}, u32[]{:S(2)}, u32[]{:S(2)}) collective-permute-start(bf16[1,64,1280]{2,1,0:T(8,128)(2,1)S(1)} %bitcast.36), channel_id=1, source_target_pairs={{0,96},{32,64},{64,32},{96,0},{128,224},{160,192},{192,160},{224,1... | collective-permute-start | bytes 491528 | tf_op jit(solution)/shard_map/ppermute | solution.py:326
  43.4 1.4 collective-permute-done.4
  44.8 3.5 %collective-permute-done.1 = bf16[128,1280]{1,0:T(8,128)(2,1)S(1)} collective-permute-done((bf16[128,1280]{1,0:T(8,128)(2,1)S(1)}, bf16[128,1280]{1,0:T(8,128)(2,1)S(1)}, u32[]{:S(2)}, u32[]{:S(2)}) %collective-permute-start.1) | collective-permute-done | bytes 327712 | tf_op jit(solution)/shard_map/ppermute | solution.py:326
  48.4 2.0 %collective-permute-start.3 = (bf16[1,64,1280]{2,1,0:T(8,128)(2,1)S(1)}, bf16[1,64,1280]{2,1,0:T(8,128)(2,1)S(1)}, u32[]{:S(2)}, u32[]{:S(2)}) collective-permute-start(bf16[1,64,1280]{2,1,0:T(8,128)(2,1)S(1)} %get-tuple-element.153), channel_id=1, source_target_pairs={{0,96},{32,64},{64,32},{96,0},{128,224},{160,192},{192,160},{224,1... | collective-permute-start | bytes 491528 | tf_op jit(solution)/shard_map/ppermute | solution.py:326
  52.0 1.8 collective-permute-done.3
  57.1 1.5 collective-permute-start.6
  59.0 3.0 %collective-permute-done.8.refs_2_.refs_6_ = bf16[2,64,1280]{2,1,0:T(8,128)(2,1)S(1)} collective-permute-done((bf16[2,64,1280]{2,1,0:T(8,128)(2,1)S(1)}, bf16[2,64,1280]{2,1,0:T(8,128)(2,1)S(1)}, u32[]{:S(2)}, u32[]{:S(2)}) %collective-permute-start.8) | collective-permute-done | bytes 327712 | tf_op jit(solution)/shard_map/ppermute | solution.py:326
  62.2 3.6 %collective-permute-done.10.refs_7_ = bf16[2688,128]{1,0:T(8,128)(2,1)S(1)} collective-permute-done((bf16[2688,128]{1,0:T(8,128)(2,1)S(1)}, bf16[2688,128]{1,0:T(8,128)(2,1)S(1)}, u32[]{:S(2)}, u32[]{:S(2)}) %collective-permute-start.10) | collective-permute-done | bytes 688160 | tf_op jit(solution)/shard_map/ppermute | solution.py:326
  65.8 2.9 %experts_partner.1 = (bf16[2,64,1280]{2,1,0:T(8,128)(2,1)S(1)}, bf16[2,64,1280]{2,1,0:T(8,128)(2,1)S(1)}, bf16[2,64,1280]{2,1,0:T(8,128)(2,1)S(1)}, bf16[2,64,12...) custom-call(s32[1]{0:T(128)} %bitcast.1.side, ...), custom_call_target="tpu_custom_call" | custom-call | flops 2013265920 | bytes 9306116 | tf_op jit(solution)/shard_map/experts_partner/pallas_call | solution.py:44
  71.1 2.9 %experts_own.1 = (bf16[2,64,1280]{2,1,0:T(8,128)(2,1)S(1)}, bf16[2,64,1280]{2,1,0:T(8,128)(2,1)S(1)}, bf16[2,64,1280]{2,1,0:T(8,128)(2,1)S(1)}, bf16[2,64,1280]{...) custom-call(s32[1]{0:T(128)} %bitcast.1.side, ...), custom_call_target="tpu_custom_call" | custom-call | flops 2013265920 | bytes 9306116 | tf_op jit(solution)/shard_map/experts_own/pallas_call | solution.py:44
  74.1 1.4 weights_given.1
  76.6 3.0 %weights_kept.1 = (bf16[2,1280,384]{2,1,0:T(8,128)(2,1)}, bf16[2,384,1280]{2,1,0:T(8,128)(2,1)}) custom-call(s32[1]{0:T(128)} %bitcast.1.side, bf16[2,64,1280]{2,1,0:T(8,128)(2,1)S(1)} %pad_maximum_fusion.2.refs_0_, bf16[2,64,1280]{2,1,0:T(8,128)(2,1)S(1)} %pad_maximum_fusion.3.refs_1_, bf16[2,64,1280]{2,1,0:T(8,128)(2,1)S(1)} %collective-permute-done.6.refs_2_, ...), custom_call_target="tpu_custom_call" | custom-call | flops 1006632960 | bytes 8126468 | tf_op jit(solution)/shard_map/weights_kept/pallas_call | solution.py:44
  79.8 1.3 collective-permute-start.18
  85.8 3.2 %collective-permute-done.13 = bf16[2,64,1280]{2,1,0:T(8,128)(2,1)S(1)} collective-permute-done((bf16[2,64,1280]{2,1,0:T(8,128)(2,1)S(1)}, bf16[2,64,1280]{2,1,0:T(8,128)(2,1)S(1)}, u32[]{:S(2)}, u32[]{:S(2)}) %collective-permute-start.13) | collective-permute-done | bytes 327712 | tf_op jit(solution)/shard_map/ppermute | solution.py:326
  90.9 1.6 collective-permute-start.16
  92.5 3.0 %collective-permute-done.15.arrived_a = bf16[64,1280]{1,0:T(8,128)(2,1)S(1)} collective-permute-done((bf16[64,1280]{1,0:T(8,128)(2,1)S(1)}, bf16[64,1280]{1,0:T(8,128)(2,1)S(1)}, u32[]{:S(2)}, u32[]{:S(2)}) %collective-permute-start.15) | collective-permute-done | bytes 163872 | tf_op jit(solution)/shard_map/ppermute | solution.py:326
  95.4 1.4 collective-permute-done.16.arrived_b
  96.9 1.3 unsort.1
  98.2 16.4 %all-to-all-start.1 = ((bf16[32,8,1280]{2,1,0:T(8,128)(2,1)}), bf16[32,8,1280]{2,1,0:T(8,128)(2,1)S(1)}, u32[]{:S(2)}, u32[]{:S(2)}) async-start(bf16[32,8,1280]{2,1,0:T(8,128)(2,1)} %bitcast.16), calls=%async_computation.1 | async-start | bytes 1310720 | tf_op jit(solution)/shard_map/all_to_all | solution.py:293
  115.1 19.5 %all-to-all-done.1 = bf16[32,8,1280]{2,1,0:T(8,128)(2,1)S(1)} async-done(((bf16[32,8,1280]{2,1,0:T(8,128)(2,1)}), bf16[32,8,1280]{2,1,0:T(8,128)(2,1)S(1)}, u32[]{:S(2)}, u32[]{:S(2)}) %all-to-all-start.1) | async-done | bytes 655392 | tf_op jit(solution)/shard_map/all_to_all | solution.py:293
  140.1 12.3 %all_to_all.26.partials = bf16[16,40,128]{2,1,0:T(8,128)(2,1)S(1)} all-to-all(bf16[16,40,128]{2,1,0:T(8,128)(2,1)S(1)} %bitcast.35), channel_id=1, replica_groups=mesh['xl'=2,'yh'=2,'yl'=2,'z'=8,'xh'=2,'c'=2] {'xl','yh','yl','xh'}, dimensions={0} | all-to-all | bytes 327680 | tf_op jit(solution)/shard_map/all_to_all | solution.py:293
  152.5 9.8 %all_to_all.27.partials = bf16[8,40,128]{2,1,0:T(8,128)(2,1)S(1)} all-to-all(bf16[8,40,128]{2,1,0:T(8,128)(2,1)S(1)} %share_plane.1), channel_id=1, replica_groups=mesh['xl'=2,'yh'=2,'yl'=2,'z'=8,'xh'=2,'c'=2] {'z'}, dimensions={0} | all-to-all | bytes 163840 | tf_op jit(solution)/shard_map/all_to_all | solution.py:293
  163.0 4.2 %all-to-all-start.4 = ((bf16[16,40,128]{2,1,0:T(8,128)(2,1)}), bf16[16,40,128]{2,1,0:T(8,128)(2,1)S(1)}, u32[]{:S(2)}, u32[]{:S(2)}) async-start(bf16[16,40,128]{2,1,0:T(8,128)(2,1)} %share_z.1), calls=%async_computation.4 | async-start | bytes 327680 | tf_op jit(solution)/shard_map/all_to_all | solution.py:293
  168.2 1.5 token_outputs.1
  169.7 1.4 merge.1
  171.1 3.2 %all-to-all-done.4.kept = bf16[16,40,128]{2,1,0:T(8,128)(2,1)S(1)} async-done(((bf16[16,40,128]{2,1,0:T(8,128)(2,1)}), bf16[16,40,128]{2,1,0:T(8,128)(2,1)S(1)}, u32[]{:S(2)}, u32[]{:S(2)}) %all-to-all-start.4) | async-done | bytes 163872 | tf_op jit(solution)/shard_map/all_to_all | solution.py:293
  174.3 4.4 %collective-permute-start.23 = (bf16[16,40,128]{2,1,0:T(8,128)(2,1)S(1)}, bf16[16,40,128]{2,1,0:T(8,128)(2,1)S(1)}, u32[]{:S(2)}, u32[]{:S(2)}) collective-permute-start(bf16[16,40,128]{2,1,0:T(8,128)(2,1)S(1)} %all-to-all-done.4.kept), channel_id=1, source_target_pairs={{0,1},{1,0},{2,3},{3,2},{4,5},{5,4},{6,7},{7,6},{8,9},{9,8},{10,11... | collective-permute-start | bytes 491528 | tf_op jit(solution)/shard_map/ppermute | solution.py:308
  (76 shorter events, 27.2 us)
Async XLA Ops:
  0.6 1.5 copy-start
  3.7 2.7 %copy-start.4 = (bf16[256,1280]{1,0:T(8,128)(2,1)S(1)}, bf16[256,1280]{1,0:T(8,128)(2,1)}, u32[]{:S(2)}) copy-start(bf16[256,1280]{1,0:T(8,128)(2,1)} %tokens.3) | copy-start | bytes 1966084
  3.7 2.7 %copy-start.6 = (bf16[256,1280]{1,0:T(8,128)(2,1)S(1)}, bf16[256,1280]{1,0:T(8,128)(2,1)}, u32[]{:S(2)}) copy-start(bf16[256,1280]{1,0:T(8,128)(2,1)} %cotangent.3) | copy-start | bytes 1966084
  3.7 2.7 %copy-start.8 = (bf16[1280,128]{1,0:T(8,128)(2,1)S(1)}, bf16[1280,128]{1,0:T(8,128)(2,1)}, u32[]{:S(2)}) copy-start(bf16[1280,128]{1,0:T(8,128)(2,1)} %router.1) | copy-start | bytes 983044
  4.2 35.4 %collective-permute-start = (bf16[4992,128]{1,0:T(8,128)(2,1)S(1)}, bf16[4992,128]{1,0:T(8,128)(2,1)S(1)}, u32[]{:S(2)}, u32[]{:S(2)}) collective-permute-start(bf16[4992,128]{1,0:T(8,128)(2,1)S(1)} %get-tuple-element.81), channel_id=1, source_target_pairs={{0,32},{32,0},{64,96},{96,64},{128,160},{160,128},{192,224},{224,1... | collective-permute-start | bytes 3833864 | tf_op jit(solution)/shard_map/ppermute | solution.py:326
  39.6 26.1 %copy-start.1 = (bf16[2,1280,384]{2,1,0:T(8,128)(2,1)S(1)}, bf16[2,1280,384]{2,1,0:T(8,128)(2,1)}, u32[]{:S(2)}) copy-start(bf16[2,1280,384]{2,1,0:T(8,128)(2,1)} %refs_4_.3) | copy-start | bytes 5898244
  39.6 26.1 %copy-start.3 = (bf16[2,384,1280]{2,1,0:T(8,128)(2,1)S(1)}, bf16[2,384,1280]{2,1,0:T(8,128)(2,1)}, u32[]{:S(2)}) copy-start(bf16[2,384,1280]{2,1,0:T(8,128)(2,1)} %refs_5_.3) | copy-start | bytes 5898244
  40.1 4.7 %collective-permute-start.4 = (bf16[1,64,1280]{2,1,0:T(8,128)(2,1)S(1)}, bf16[1,64,1280]{2,1,0:T(8,128)(2,1)S(1)}, u32[]{:S(2)}, u32[]{:S(2)}) collective-permute-start(bf16[1,64,1280]{2,1,0:T(8,128)(2,1)S(1)} %bitcast.38), channel_id=1, source_target_pairs={{0,128},{32,160},{64,192},{96,224},{128,0},{160,32},{192,64},{224,... | collective-permute-start | bytes 491528 | tf_op jit(solution)/shard_map/ppermute | solution.py:326
  40.5 7.9 %collective-permute-start.1 = (bf16[128,1280]{1,0:T(8,128)(2,1)S(1)}, bf16[128,1280]{1,0:T(8,128)(2,1)S(1)}, u32[]{:S(2)}, u32[]{:S(2)}) collective-permute-start(bf16[128,1280]{1,0:T(8,128)(2,1)S(1)} %get-tuple-element.83), channel_id=1, source_target_pairs={{0,32},{32,0},{64,96},{96,64},{128,160},{160,128},{192,224},{224,1... | collective-permute-start | bytes 983048 | tf_op jit(solution)/shard_map/ppermute | solution.py:326
  41.0 9.4 %collective-permute-start.5 = (bf16[1,64,1280]{2,1,0:T(8,128)(2,1)S(1)}, bf16[1,64,1280]{2,1,0:T(8,128)(2,1)S(1)}, u32[]{:S(2)}, u32[]{:S(2)}) collective-permute-start(bf16[1,64,1280]{2,1,0:T(8,128)(2,1)S(1)} %bitcast.36), channel_id=1, source_target_pairs={{0,96},{32,64},{64,32},{96,0},{128,224},{160,192},{192,160},{224,1... | collective-permute-start | bytes 491528 | tf_op jit(solution)/shard_map/ppermute | solution.py:326
  48.4 5.5 %collective-permute-start.3 = (bf16[1,64,1280]{2,1,0:T(8,128)(2,1)S(1)}, bf16[1,64,1280]{2,1,0:T(8,128)(2,1)S(1)}, u32[]{:S(2)}, u32[]{:S(2)}) collective-permute-start(bf16[1,64,1280]{2,1,0:T(8,128)(2,1)S(1)} %get-tuple-element.153), channel_id=1, source_target_pairs={{0,96},{32,64},{64,32},{96,0},{128,224},{160,192},{192,160},{224,1... | collective-permute-start | bytes 491528 | tf_op jit(solution)/shard_map/ppermute | solution.py:326
  50.4 4.3 %collective-permute-start.2 = (bf16[1,64,1280]{2,1,0:T(8,128)(2,1)S(1)}, bf16[1,64,1280]{2,1,0:T(8,128)(2,1)S(1)}, u32[]{:S(2)}, u32[]{:S(2)}) collective-permute-start(bf16[1,64,1280]{2,1,0:T(8,128)(2,1)S(1)} %get-tuple-element.154), channel_id=1, source_target_pairs={{0,128},{32,160},{64,192},{96,224},{128,0},{160,32},{192,64},{224,... | collective-permute-start | bytes 491528 | tf_op jit(solution)/shard_map/ppermute | solution.py:326
  51.7 14.1 %collective-permute-start.10 = (bf16[2688,128]{1,0:T(8,128)(2,1)S(1)}, bf16[2688,128]{1,0:T(8,128)(2,1)S(1)}, u32[]{:S(2)}, u32[]{:S(2)}) collective-permute-start(bf16[2688,128]{1,0:T(8,128)(2,1)S(1)} %get-tuple-element.96), channel_id=1, source_target_pairs={{0,32},{32,0},{64,96},{96,64},{128,160},{160,128},{192,224},{224,1... | collective-permute-start | bytes 2064392 | tf_op jit(solution)/shard_map/ppermute | solution.py:326
  54.7 7.2 %collective-permute-start.8 = (bf16[2,64,1280]{2,1,0:T(8,128)(2,1)S(1)}, bf16[2,64,1280]{2,1,0:T(8,128)(2,1)S(1)}, u32[]{:S(2)}, u32[]{:S(2)}) collective-permute-start(bf16[2,64,1280]{2,1,0:T(8,128)(2,1)S(1)} %pad_maximum_fusion.refs_0_.refs_4_), channel_id=1, source_target_pairs={{0,96},{32,64},{64,32},{96,0},{128,224},{160,192},{192,160},{224,1... | collective-permute-start | bytes 983048 | tf_op jit(solution)/shard_map/ppermute | solution.py:326
  55.9 6.2 %collective-permute-start.9 = (bf16[2,64,1280]{2,1,0:T(8,128)(2,1)S(1)}, bf16[2,64,1280]{2,1,0:T(8,128)(2,1)S(1)}, u32[]{:S(2)}, u32[]{:S(2)}) collective-permute-start(bf16[2,64,1280]{2,1,0:T(8,128)(2,1)S(1)} %pad_maximum_fusion.1.refs_1_.refs_5_), channel_id=1, source_target_pairs={{0,128},{32,160},{64,192},{96,224},{128,0},{160,32},{192,64},{224,... | collective-permute-start | bytes 983048 | tf_op jit(solution)/shard_map/ppermute | solution.py:326
  57.1 11.6 %collective-permute-start.6 = (bf16[2,64,1280]{2,1,0:T(8,128)(2,1)S(1)}, bf16[2,64,1280]{2,1,0:T(8,128)(2,1)S(1)}, u32[]{:S(2)}, u32[]{:S(2)}) collective-permute-start(bf16[2,64,1280]{2,1,0:T(8,128)(2,1)S(1)} %pad_maximum_fusion.2.refs_0_), channel_id=1, source_target_pairs={{0,96},{32,64},{64,32},{96,0},{128,224},{160,192},{192,160},{224,1... | collective-permute-start | bytes 983048 | tf_op jit(solution)/shard_map/ppermute | solution.py:326
  58.6 10.1 %collective-permute-start.7 = (bf16[2,64,1280]{2,1,0:T(8,128)(2,1)S(1)}, bf16[2,64,1280]{2,1,0:T(8,128)(2,1)S(1)}, u32[]{:S(2)}, u32[]{:S(2)}) collective-permute-start(bf16[2,64,1280]{2,1,0:T(8,128)(2,1)S(1)} %pad_maximum_fusion.3.refs_1_), channel_id=1, source_target_pairs={{0,128},{32,160},{64,192},{96,224},{128,0},{160,32},{192,64},{224,... | collective-permute-start | bytes 983048 | tf_op jit(solution)/shard_map/ppermute | solution.py:326
  68.7 10.9 %collective-permute-start.11 = (bf16[2,64,1280]{2,1,0:T(8,128)(2,1)S(1)}, bf16[2,64,1280]{2,1,0:T(8,128)(2,1)S(1)}, u32[]{:S(2)}, u32[]{:S(2)}) collective-permute-start(bf16[2,64,1280]{2,1,0:T(8,128)(2,1)S(1)} %get-tuple-element.102), channel_id=1, source_target_pairs={{0,96},{32,64},{64,32},{96,0},{128,224},{160,192},{192,160},{224,1... | collective-permute-start | bytes 983048 | tf_op jit(solution)/shard_map/ppermute | solution.py:326
  70.0 9.7 %collective-permute-start.12 = (bf16[2,64,1280]{2,1,0:T(8,128)(2,1)S(1)}, bf16[2,64,1280]{2,1,0:T(8,128)(2,1)S(1)}, u32[]{:S(2)}, u32[]{:S(2)}) collective-permute-start(bf16[2,64,1280]{2,1,0:T(8,128)(2,1)S(1)} %get-tuple-element.104), channel_id=1, source_target_pairs={{0,128},{32,160},{64,192},{96,224},{128,0},{160,32},{192,64},{224,... | collective-permute-start | bytes 983048 | tf_op jit(solution)/shard_map/ppermute | solution.py:326
  76.6 14.1 %collective-permute-start.19 = (bf16[2560,128]{1,0:T(8,128)(2,1)S(1)}, bf16[2560,128]{1,0:T(8,128)(2,1)S(1)}, u32[]{:S(2)}, u32[]{:S(2)}) collective-permute-start(bf16[2560,128]{1,0:T(8,128)(2,1)S(1)} %get-tuple-element.127), channel_id=1, source_target_pairs={{0,32},{32,0},{64,96},{96,64},{128,160},{160,128},{192,224},{224,1... | collective-permute-start | bytes 1966088 | tf_op jit(solution)/shard_map/ppermute | solution.py:326
  79.8 5.5 %collective-permute-start.18 = (bf16[64,1280]{1,0:T(8,128)(2,1)S(1)}, bf16[64,1280]{1,0:T(8,128)(2,1)S(1)}, u32[]{:S(2)}, u32[]{:S(2)}) collective-permute-start(bf16[64,1280]{1,0:T(8,128)(2,1)S(1)} %slice_bitcast_fusion), channel_id=1, source_target_pairs={{0,96},{32,64},{64,32},{96,0},{128,224},{160,192},{192,160},{224,1... | collective-permute-start | bytes 491528 | tf_op jit(solution)/shard_map/ppermute | solution.py:326
  81.2 4.6 %collective-permute-start.17 = (bf16[64,1280]{1,0:T(8,128)(2,1)S(1)}, bf16[64,1280]{1,0:T(8,128)(2,1)S(1)}, u32[]{:S(2)}, u32[]{:S(2)}) collective-permute-start(bf16[64,1280]{1,0:T(8,128)(2,1)S(1)} %slice_bitcast_fusion.1), channel_id=1, source_target_pairs={{0,128},{32,160},{64,192},{96,224},{128,0},{160,32},{192,64},{224,... | collective-permute-start | bytes 491528 | tf_op jit(solution)/shard_map/ppermute | solution.py:326
  81.9 7.1 %collective-permute-start.13 = (bf16[2,64,1280]{2,1,0:T(8,128)(2,1)S(1)}, bf16[2,64,1280]{2,1,0:T(8,128)(2,1)S(1)}, u32[]{:S(2)}, u32[]{:S(2)}) collective-permute-start(bf16[2,64,1280]{2,1,0:T(8,128)(2,1)S(1)} %get-tuple-element.112), channel_id=1, source_target_pairs={{0,96},{32,64},{64,32},{96,0},{128,224},{160,192},{192,160},{224,1... | collective-permute-start | bytes 983048 | tf_op jit(solution)/shard_map/ppermute | solution.py:326
  83.0 6.2 %collective-permute-start.14 = (bf16[2,64,1280]{2,1,0:T(8,128)(2,1)S(1)}, bf16[2,64,1280]{2,1,0:T(8,128)(2,1)S(1)}, u32[]{:S(2)}, u32[]{:S(2)}) collective-permute-start(bf16[2,64,1280]{2,1,0:T(8,128)(2,1)S(1)} %get-tuple-element.114), channel_id=1, source_target_pairs={{0,128},{32,160},{64,192},{96,224},{128,0},{160,32},{192,64},{224,... | collective-permute-start | bytes 983048 | tf_op jit(solution)/shard_map/ppermute | solution.py:326
  89.4 6.1 %collective-permute-start.15 = (bf16[64,1280]{1,0:T(8,128)(2,1)S(1)}, bf16[64,1280]{1,0:T(8,128)(2,1)S(1)}, u32[]{:S(2)}, u32[]{:S(2)}) collective-permute-start(bf16[64,1280]{1,0:T(8,128)(2,1)S(1)} %get-tuple-element.151), channel_id=1, source_target_pairs={{0,128},{32,160},{64,192},{96,224},{128,0},{160,32},{192,64},{224,... | collective-permute-start | bytes 491528 | tf_op jit(solution)/shard_map/ppermute | solution.py:326
  90.7 6.2 %collective-permute-start.20 = (bf16[128,1280]{1,0:T(8,128)(2,1)S(1)}, bf16[128,1280]{1,0:T(8,128)(2,1)S(1)}, u32[]{:S(2)}, u32[]{:S(2)}) collective-permute-start(bf16[128,1280]{1,0:T(8,128)(2,1)S(1)} %pad_maximum_fusion.4), channel_id=1, source_target_pairs={{0,32},{32,0},{64,96},{96,64},{128,160},{160,128},{192,224},{224,1... | collective-permute-start | bytes 983048 | tf_op jit(solution)/shard_map/ppermute | solution.py:326
  90.9 6.0 %collective-permute-start.16 = (bf16[64,1280]{1,0:T(8,128)(2,1)S(1)}, bf16[64,1280]{1,0:T(8,128)(2,1)S(1)}, u32[]{:S(2)}, u32[]{:S(2)}) collective-permute-start(bf16[64,1280]{1,0:T(8,128)(2,1)S(1)} %get-tuple-element.149), channel_id=1, source_target_pairs={{0,96},{32,64},{64,32},{96,0},{128,224},{160,192},{192,160},{224,1... | collective-permute-start | bytes 491528 | tf_op jit(solution)/shard_map/ppermute | solution.py:326
  98.2 36.3 %all-to-all-start.1 = ((bf16[32,8,1280]{2,1,0:T(8,128)(2,1)}), bf16[32,8,1280]{2,1,0:T(8,128)(2,1)S(1)}, u32[]{:S(2)}, u32[]{:S(2)}) async-start(bf16[32,8,1280]{2,1,0:T(8,128)(2,1)} %bitcast.16), calls=%async_computation.1 | async-start | bytes 1310720 | tf_op jit(solution)/shard_map/all_to_all | solution.py:293
  114.7 55.0 %collective-permute-start.22 = (bf16[5120,128]{1,0:T(8,128)(2,1)}, bf16[5120,128]{1,0:T(8,128)(2,1)S(1)}, u32[]{:S(2)}, u32[]{:S(2)}) collective-permute-start(bf16[5120,128]{1,0:T(8,128)(2,1)} %copy-done.10), channel_id=1, source_target_pairs={{0,32},{32,0},{64,96},{96,64},{128,160},{160,128},{192,224},{224,1... | collective-permute-start | bytes 3932168 | tf_op jit(solution)/shard_map/ppermute | solution.py:326
  137.9 2.2 %collective-permute-start.21 = (bf16[640,128]{1,0:T(8,128)(2,1)S(1)}, bf16[640,128]{1,0:T(8,128)(2,1)S(1)}, u32[]{:S(2)}, u32[]{:S(2)}) collective-permute-start(bf16[640,128]{1,0:T(8,128)(2,1)S(1)} %get-tuple-element.134), channel_id=1, source_target_pairs={{0,1},{1,0},{2,3},{3,2},{4,5},{5,4},{6,7},{7,6},{8,9},{9,8},{10,11... | collective-permute-start | bytes 491528 | tf_op jit(solution)/shard_map/ppermute | solution.py:301
  163.0 11.3 %all-to-all-start.4 = ((bf16[16,40,128]{2,1,0:T(8,128)(2,1)}), bf16[16,40,128]{2,1,0:T(8,128)(2,1)S(1)}, u32[]{:S(2)}, u32[]{:S(2)}) async-start(bf16[16,40,128]{2,1,0:T(8,128)(2,1)} %share_z.1), calls=%async_computation.4 | async-start | bytes 327680 | tf_op jit(solution)/shard_map/all_to_all | solution.py:293
  174.3 5.4 %collective-permute-start.23 = (bf16[16,40,128]{2,1,0:T(8,128)(2,1)S(1)}, bf16[16,40,128]{2,1,0:T(8,128)(2,1)S(1)}, u32[]{:S(2)}, u32[]{:S(2)}) collective-permute-start(bf16[16,40,128]{2,1,0:T(8,128)(2,1)S(1)} %all-to-all-done.4.kept), channel_id=1, source_target_pairs={{0,1},{1,0},{2,3},{3,2},{4,5},{5,4},{6,7},{7,6},{8,9},{9,8},{10,11... | collective-permute-start | bytes 491528 | tf_op jit(solution)/shard_map/ppermute | solution.py:308
  (5 other events, 5.8 us)

commit v4 on v3

--- a/solution.py
+++ b/solution.py
@@ -418,10 +418,10 @@
     partner_sum = first_sum(*partner_done)
     partner_sum, own_done = tied((partner_sum, own_done))
     partner_sum, _ = second_sum(*partner_sum, ())
-    own_sum, mine = second_sum(*first_sum(*own_done), mine)
+    own_sum, _ = second_sum(*first_sum(*own_done), ())
     a, arrived_a, b, arrived_b = partner_sum
     ready = jnp.concatenate([add(a, arrived_a), add(b, arrived_b)], axis=0)
-    ready, received = tied((ready, received))
+    ready, received, mine = tied((ready, received, mine))
     returned = exchange(ready, "y1")
     back = call(
         unsort_kernel,

time: 181 us -> 181 us (level)
  no operation moved by 1% of the time
where the time goes in v4:
time: 181 us
  blocking collectives  53.9 us (30%)
  starting transfers between devices  49.7 us (27%)
  waiting for transfers between devices  48.4 us (27%)
  Pallas kernels  19.7 us (11%)
  local copies, waits for them, and re-layouts  7.43 us (4%)
    all_to_all x3, blocking collectives, swap(): return lax.all_to_all(value, axis, split_axis=0, concat_axis=0, tiled=True)  53.9 us
    ppermute x22, waiting for transfers between devices, exchange(): return lax.ppermute(value, DP, neighbour(dim))  23.7 us
    ppermute x22, starting transfers between devices, exchange(): return lax.ppermute(value, DP, neighbour(dim))  23.6 us
    all_to_all x2, waiting for transfers between devices, swap(): return lax.all_to_all(value, axis, split_axis=0, concat_axis=0, tiled=True)  22.7 us
    all_to_all x2, starting transfers between devices, swap(): return lax.all_to_all(value, axis, split_axis=0, concat_axis=0, tiled=True)  20.6 us
    pallas_call x15, Pallas kernels, call(): pl.pallas_call(kernel, out_shape=out_shape, in_specs=[smem if a.dtype ==...  19.7 us
    unnamed x22, local copies, waits for them, and re-layouts  7.34 us
    ppermute x1, starting transfers between devices, sum_router(): received = lax.ppermute(share, 'c', CORES)  4.35 us
  transfers between devices with their start and end apart: 26, of which 17 were waited for; matrix products, arithmetic and copies ran while one was open for 0% of the time, Pallas kernels for 9%

profile of v4, /device:TPU:1, one launch (start us, length us, event | category | flops | bytes accessed | tf_op | source)
XLA Modules:
  0.0 180.6 jit_solution(12957265412244345821)
XLA Ops:
  0.7 1.5 copy-done
  2.2 1.5 copy-done.2
  4.2 2.2 %collective-permute-start = (bf16[4992,128]{1,0:T(8,128)(2,1)S(1)}, bf16[4992,128]{1,0:T(8,128)(2,1)S(1)}, u32[]{:S(2)}, u32[]{:S(2)}) collective-permute-start(bf16[4992,128]{1,0:T(8,128)(2,1)S(1)} %get-tuple-element.81), channel_id=1, source_target_pairs={{0,32},{32,0},{64,96},{96,64},{128,160},{160,128},{192,224},{224,1... | collective-permute-start | bytes 3833864 | tf_op jit(solution)/shard_map/ppermute | solution.py:326
  6.5 1.4 prologue.1
  7.9 31.7 %all_to_all.25 = bf16[32,8,1280]{2,1,0:T(8,128)(2,1)S(1)} all-to-all(bf16[32,8,1280]{2,1,0:T(8,128)(2,1)S(1)} %bitcast.34), channel_id=1, replica_groups=mesh['xl'=2,'yh'=2,'yl'=2,'z'=8,'xh'=2,'c'=2] {'z','xh','c'}, dimensions={0} | all-to-all | bytes 1310720 | tf_op jit(solution)/shard_map/all_to_all | solution.py:293
  41.0 2.4 %collective-permute-start.5 = (bf16[1,64,1280]{2,1,0:T(8,128)(2,1)S(1)}, bf16[1,64,1280]{2,1,0:T(8,128)(2,1)S(1)}, u32[]{:S(2)}, u32[]{:S(2)}) collective-permute-start(bf16[1,64,1280]{2,1,0:T(8,128)(2,1)S(1)} %bitcast.36), channel_id=1, source_target_pairs={{0,96},{32,64},{64,32},{96,0},{128,224},{160,192},{192,160},{224,1... | collective-permute-start | bytes 491528 | tf_op jit(solution)/shard_map/ppermute | solution.py:326
  43.4 1.4 collective-permute-done.4
  44.8 3.5 %collective-permute-done.1 = bf16[128,1280]{1,0:T(8,128)(2,1)S(1)} collective-permute-done((bf16[128,1280]{1,0:T(8,128)(2,1)S(1)}, bf16[128,1280]{1,0:T(8,128)(2,1)S(1)}, u32[]{:S(2)}, u32[]{:S(2)}) %collective-permute-start.1) | collective-permute-done | bytes 327712 | tf_op jit(solution)/shard_map/ppermute | solution.py:326
  48.4 2.0 %collective-permute-start.3 = (bf16[1,64,1280]{2,1,0:T(8,128)(2,1)S(1)}, bf16[1,64,1280]{2,1,0:T(8,128)(2,1)S(1)}, u32[]{:S(2)}, u32[]{:S(2)}) collective-permute-start(bf16[1,64,1280]{2,1,0:T(8,128)(2,1)S(1)} %get-tuple-element.153), channel_id=1, source_target_pairs={{0,96},{32,64},{64,32},{96,0},{128,224},{160,192},{192,160},{224,1... | collective-permute-start | bytes 491528 | tf_op jit(solution)/shard_map/ppermute | solution.py:326
  52.0 1.8 collective-permute-done.3
  57.1 1.5 collective-permute-start.6
  59.0 3.0 %collective-permute-done.8.refs_2_.refs_6_ = bf16[2,64,1280]{2,1,0:T(8,128)(2,1)S(1)} collective-permute-done((bf16[2,64,1280]{2,1,0:T(8,128)(2,1)S(1)}, bf16[2,64,1280]{2,1,0:T(8,128)(2,1)S(1)}, u32[]{:S(2)}, u32[]{:S(2)}) %collective-permute-start.8) | collective-permute-done | bytes 327712 | tf_op jit(solution)/shard_map/ppermute | solution.py:326
  62.2 3.6 %collective-permute-done.10.refs_7_ = bf16[2688,128]{1,0:T(8,128)(2,1)S(1)} collective-permute-done((bf16[2688,128]{1,0:T(8,128)(2,1)S(1)}, bf16[2688,128]{1,0:T(8,128)(2,1)S(1)}, u32[]{:S(2)}, u32[]{:S(2)}) %collective-permute-start.10) | collective-permute-done | bytes 688160 | tf_op jit(solution)/shard_map/ppermute | solution.py:326
  65.8 2.9 %experts_partner.1 = (bf16[2,64,1280]{2,1,0:T(8,128)(2,1)S(1)}, bf16[2,64,1280]{2,1,0:T(8,128)(2,1)S(1)}, bf16[2,64,1280]{2,1,0:T(8,128)(2,1)S(1)}, bf16[2,64,12...) custom-call(s32[1]{0:T(128)} %bitcast.1.side, ...), custom_call_target="tpu_custom_call" | custom-call | flops 2013265920 | bytes 9306116 | tf_op jit(solution)/shard_map/experts_partner/pallas_call | solution.py:44
  71.1 2.9 %experts_own.1 = (bf16[2,64,1280]{2,1,0:T(8,128)(2,1)S(1)}, bf16[2,64,1280]{2,1,0:T(8,128)(2,1)S(1)}, bf16[2,64,1280]{2,1,0:T(8,128)(2,1)S(1)}, bf16[2,64,1280]{...) custom-call(s32[1]{0:T(128)} %bitcast.1.side, ...), custom_call_target="tpu_custom_call" | custom-call | flops 2013265920 | bytes 9306116 | tf_op jit(solution)/shard_map/experts_own/pallas_call | solution.py:44
  74.1 1.4 weights_given.1
  76.6 3.0 %weights_kept.1 = (bf16[2,1280,384]{2,1,0:T(8,128)(2,1)}, bf16[2,384,1280]{2,1,0:T(8,128)(2,1)}) custom-call(s32[1]{0:T(128)} %bitcast.1.side, bf16[2,64,1280]{2,1,0:T(8,128)(2,1)S(1)} %pad_maximum_fusion.2.refs_0_, bf16[2,64,1280]{2,1,0:T(8,128)(2,1)S(1)} %pad_maximum_fusion.3.refs_1_, bf16[2,64,1280]{2,1,0:T(8,128)(2,1)S(1)} %collective-permute-done.6.refs_2_, ...), custom_call_target="tpu_custom_call" | custom-call | flops 1006632960 | bytes 8126468 | tf_op jit(solution)/shard_map/weights_kept/pallas_call | solution.py:44
  79.8 1.3 collective-permute-start.18
  85.8 3.2 %collective-permute-done.13 = bf16[2,64,1280]{2,1,0:T(8,128)(2,1)S(1)} collective-permute-done((bf16[2,64,1280]{2,1,0:T(8,128)(2,1)S(1)}, bf16[2,64,1280]{2,1,0:T(8,128)(2,1)S(1)}, u32[]{:S(2)}, u32[]{:S(2)}) %collective-permute-start.13) | collective-permute-done | bytes 327712 | tf_op jit(solution)/shard_map/ppermute | solution.py:326
  90.9 1.6 collective-permute-start.16
  92.5 3.0 %collective-permute-done.15.arrived_a = bf16[64,1280]{1,0:T(8,128)(2,1)S(1)} collective-permute-done((bf16[64,1280]{1,0:T(8,128)(2,1)S(1)}, bf16[64,1280]{1,0:T(8,128)(2,1)S(1)}, u32[]{:S(2)}, u32[]{:S(2)}) %collective-permute-start.15) | collective-permute-done | bytes 163872 | tf_op jit(solution)/shard_map/ppermute | solution.py:326
  95.4 1.4 collective-permute-done.16.arrived_b
  96.9 1.3 unsort.1
  98.2 16.4 %all-to-all-start.1 = ((bf16[32,8,1280]{2,1,0:T(8,128)(2,1)}), bf16[32,8,1280]{2,1,0:T(8,128)(2,1)S(1)}, u32[]{:S(2)}, u32[]{:S(2)}) async-start(bf16[32,8,1280]{2,1,0:T(8,128)(2,1)} %bitcast.16), calls=%async_computation.1 | async-start | bytes 1310720 | tf_op jit(solution)/shard_map/all_to_all | solution.py:293
  115.1 19.5 %all-to-all-done.1 = bf16[32,8,1280]{2,1,0:T(8,128)(2,1)S(1)} async-done(((bf16[32,8,1280]{2,1,0:T(8,128)(2,1)}), bf16[32,8,1280]{2,1,0:T(8,128)(2,1)S(1)}, u32[]{:S(2)}, u32[]{:S(2)}) %all-to-all-start.1) | async-done | bytes 655392 | tf_op jit(solution)/shard_map/all_to_all | solution.py:293
  140.1 12.3 %all_to_all.26.partials = bf16[16,40,128]{2,1,0:T(8,128)(2,1)S(1)} all-to-all(bf16[16,40,128]{2,1,0:T(8,128)(2,1)S(1)} %bitcast.35), channel_id=1, replica_groups=mesh['xl'=2,'yh'=2,'yl'=2,'z'=8,'xh'=2,'c'=2] {'xl','yh','yl','xh'}, dimensions={0} | all-to-all | bytes 327680 | tf_op jit(solution)/shard_map/all_to_all | solution.py:293
  152.5 9.8 %all_to_all.27.partials = bf16[8,40,128]{2,1,0:T(8,128)(2,1)S(1)} all-to-all(bf16[8,40,128]{2,1,0:T(8,128)(2,1)S(1)} %share_plane.1), channel_id=1, replica_groups=mesh['xl'=2,'yh'=2,'yl'=2,'z'=8,'xh'=2,'c'=2] {'z'}, dimensions={0} | all-to-all | bytes 163840 | tf_op jit(solution)/shard_map/all_to_all | solution.py:293
  163.0 4.2 %all-to-all-start.4 = ((bf16[16,40,128]{2,1,0:T(8,128)(2,1)}), bf16[16,40,128]{2,1,0:T(8,128)(2,1)S(1)}, u32[]{:S(2)}, u32[]{:S(2)}) async-start(bf16[16,40,128]{2,1,0:T(8,128)(2,1)} %share_z.1), calls=%async_computation.4 | async-start | bytes 327680 | tf_op jit(solution)/shard_map/all_to_all | solution.py:293
  168.2 1.5 token_outputs.1
  169.7 1.4 merge.1
  171.1 3.2 %all-to-all-done.4.kept = bf16[16,40,128]{2,1,0:T(8,128)(2,1)S(1)} async-done(((bf16[16,40,128]{2,1,0:T(8,128)(2,1)}), bf16[16,40,128]{2,1,0:T(8,128)(2,1)S(1)}, u32[]{:S(2)}, u32[]{:S(2)}) %all-to-all-start.4) | async-done | bytes 163872 | tf_op jit(solution)/shard_map/all_to_all | solution.py:293
  174.3 4.4 %collective-permute-start.23 = (bf16[16,40,128]{2,1,0:T(8,128)(2,1)S(1)}, bf16[16,40,128]{2,1,0:T(8,128)(2,1)S(1)}, u32[]{:S(2)}, u32[]{:S(2)}) collective-permute-start(bf16[16,40,128]{2,1,0:T(8,128)(2,1)S(1)} %all-to-all-done.4.kept), channel_id=1, source_target_pairs={{0,1},{1,0},{2,3},{3,2},{4,5},{5,4},{6,7},{7,6},{8,9},{9,8},{10,11... | collective-permute-start | bytes 491528 | tf_op jit(solution)/shard_map/ppermute | solution.py:308
  (76 shorter events, 27.2 us)
Async XLA Ops:
  0.6 1.5 copy-start
  3.7 2.7 %copy-start.4 = (bf16[256,1280]{1,0:T(8,128)(2,1)S(1)}, bf16[256,1280]{1,0:T(8,128)(2,1)}, u32[]{:S(2)}) copy-start(bf16[256,1280]{1,0:T(8,128)(2,1)} %tokens.3) | copy-start | bytes 1966084
  3.7 2.7 %copy-start.6 = (bf16[256,1280]{1,0:T(8,128)(2,1)S(1)}, bf16[256,1280]{1,0:T(8,128)(2,1)}, u32[]{:S(2)}) copy-start(bf16[256,1280]{1,0:T(8,128)(2,1)} %cotangent.3) | copy-start | bytes 1966084
  3.7 2.7 %copy-start.8 = (bf16[1280,128]{1,0:T(8,128)(2,1)S(1)}, bf16[1280,128]{1,0:T(8,128)(2,1)}, u32[]{:S(2)}) copy-start(bf16[1280,128]{1,0:T(8,128)(2,1)} %router.1) | copy-start | bytes 983044
  4.2 35.4 %collective-permute-start = (bf16[4992,128]{1,0:T(8,128)(2,1)S(1)}, bf16[4992,128]{1,0:T(8,128)(2,1)S(1)}, u32[]{:S(2)}, u32[]{:S(2)}) collective-permute-start(bf16[4992,128]{1,0:T(8,128)(2,1)S(1)} %get-tuple-element.81), channel_id=1, source_target_pairs={{0,32},{32,0},{64,96},{96,64},{128,160},{160,128},{192,224},{224,1... | collective-permute-start | bytes 3833864 | tf_op jit(solution)/shard_map/ppermute | solution.py:326
  39.6 26.1 %copy-start.1 = (bf16[2,1280,384]{2,1,0:T(8,128)(2,1)S(1)}, bf16[2,1280,384]{2,1,0:T(8,128)(2,1)}, u32[]{:S(2)}) copy-start(bf16[2,1280,384]{2,1,0:T(8,128)(2,1)} %refs_4_.3) | copy-start | bytes 5898244
  39.6 26.1 %copy-start.3 = (bf16[2,384,1280]{2,1,0:T(8,128)(2,1)S(1)}, bf16[2,384,1280]{2,1,0:T(8,128)(2,1)}, u32[]{:S(2)}) copy-start(bf16[2,384,1280]{2,1,0:T(8,128)(2,1)} %refs_5_.3) | copy-start | bytes 5898244
  40.1 4.7 %collective-permute-start.4 = (bf16[1,64,1280]{2,1,0:T(8,128)(2,1)S(1)}, bf16[1,64,1280]{2,1,0:T(8,128)(2,1)S(1)}, u32[]{:S(2)}, u32[]{:S(2)}) collective-permute-start(bf16[1,64,1280]{2,1,0:T(8,128)(2,1)S(1)} %bitcast.38), channel_id=1, source_target_pairs={{0,128},{32,160},{64,192},{96,224},{128,0},{160,32},{192,64},{224,... | collective-permute-start | bytes 491528 | tf_op jit(solution)/shard_map/ppermute | solution.py:326
  40.5 7.9 %collective-permute-start.1 = (bf16[128,1280]{1,0:T(8,128)(2,1)S(1)}, bf16[128,1280]{1,0:T(8,128)(2,1)S(1)}, u32[]{:S(2)}, u32[]{:S(2)}) collective-permute-start(bf16[128,1280]{1,0:T(8,128)(2,1)S(1)} %get-tuple-element.83), channel_id=1, source_target_pairs={{0,32},{32,0},{64,96},{96,64},{128,160},{160,128},{192,224},{224,1... | collective-permute-start | bytes 983048 | tf_op jit(solution)/shard_map/ppermute | solution.py:326
  41.0 9.4 %collective-permute-start.5 = (bf16[1,64,1280]{2,1,0:T(8,128)(2,1)S(1)}, bf16[1,64,1280]{2,1,0:T(8,128)(2,1)S(1)}, u32[]{:S(2)}, u32[]{:S(2)}) collective-permute-start(bf16[1,64,1280]{2,1,0:T(8,128)(2,1)S(1)} %bitcast.36), channel_id=1, source_target_pairs={{0,96},{32,64},{64,32},{96,0},{128,224},{160,192},{192,160},{224,1... | collective-permute-start | bytes 491528 | tf_op jit(solution)/shard_map/ppermute | solution.py:326
  48.4 5.5 %collective-permute-start.3 = (bf16[1,64,1280]{2,1,0:T(8,128)(2,1)S(1)}, bf16[1,64,1280]{2,1,0:T(8,128)(2,1)S(1)}, u32[]{:S(2)}, u32[]{:S(2)}) collective-permute-start(bf16[1,64,1280]{2,1,0:T(8,128)(2,1)S(1)} %get-tuple-element.153), channel_id=1, source_target_pairs={{0,96},{32,64},{64,32},{96,0},{128,224},{160,192},{192,160},{224,1... | collective-permute-start | bytes 491528 | tf_op jit(solution)/shard_map/ppermute | solution.py:326
  50.4 4.3 %collective-permute-start.2 = (bf16[1,64,1280]{2,1,0:T(8,128)(2,1)S(1)}, bf16[1,64,1280]{2,1,0:T(8,128)(2,1)S(1)}, u32[]{:S(2)}, u32[]{:S(2)}) collective-permute-start(bf16[1,64,1280]{2,1,0:T(8,128)(2,1)S(1)} %get-tuple-element.154), channel_id=1, source_target_pairs={{0,128},{32,160},{64,192},{96,224},{128,0},{160,32},{192,64},{224,... | collective-permute-start | bytes 491528 | tf_op jit(solution)/shard_map/ppermute | solution.py:326
  51.7 14.1 %collective-permute-start.10 = (bf16[2688,128]{1,0:T(8,128)(2,1)S(1)}, bf16[2688,128]{1,0:T(8,128)(2,1)S(1)}, u32[]{:S(2)}, u32[]{:S(2)}) collective-permute-start(bf16[2688,128]{1,0:T(8,128)(2,1)S(1)} %get-tuple-element.96), channel_id=1, source_target_pairs={{0,32},{32,0},{64,96},{96,64},{128,160},{160,128},{192,224},{224,1... | collective-permute-start | bytes 2064392 | tf_op jit(solution)/shard_map/ppermute | solution.py:326
  54.7 7.2 %collective-permute-start.8 = (bf16[2,64,1280]{2,1,0:T(8,128)(2,1)S(1)}, bf16[2,64,1280]{2,1,0:T(8,128)(2,1)S(1)}, u32[]{:S(2)}, u32[]{:S(2)}) collective-permute-start(bf16[2,64,1280]{2,1,0:T(8,128)(2,1)S(1)} %pad_maximum_fusion.refs_0_.refs_4_), channel_id=1, source_target_pairs={{0,96},{32,64},{64,32},{96,0},{128,224},{160,192},{192,160},{224,1... | collective-permute-start | bytes 983048 | tf_op jit(solution)/shard_map/ppermute | solution.py:326
  55.9 6.2 %collective-permute-start.9 = (bf16[2,64,1280]{2,1,0:T(8,128)(2,1)S(1)}, bf16[2,64,1280]{2,1,0:T(8,128)(2,1)S(1)}, u32[]{:S(2)}, u32[]{:S(2)}) collective-permute-start(bf16[2,64,1280]{2,1,0:T(8,128)(2,1)S(1)} %pad_maximum_fusion.1.refs_1_.refs_5_), channel_id=1, source_target_pairs={{0,128},{32,160},{64,192},{96,224},{128,0},{160,32},{192,64},{224,... | collective-permute-start | bytes 983048 | tf_op jit(solution)/shard_map/ppermute | solution.py:326
  57.1 11.6 %collective-permute-start.6 = (bf16[2,64,1280]{2,1,0:T(8,128)(2,1)S(1)}, bf16[2,64,1280]{2,1,0:T(8,128)(2,1)S(1)}, u32[]{:S(2)}, u32[]{:S(2)}) collective-permute-start(bf16[2,64,1280]{2,1,0:T(8,128)(2,1)S(1)} %pad_maximum_fusion.2.refs_0_), channel_id=1, source_target_pairs={{0,96},{32,64},{64,32},{96,0},{128,224},{160,192},{192,160},{224,1... | collective-permute-start | bytes 983048 | tf_op jit(solution)/shard_map/ppermute | solution.py:326
  58.6 10.1 %collective-permute-start.7 = (bf16[2,64,1280]{2,1,0:T(8,128)(2,1)S(1)}, bf16[2,64,1280]{2,1,0:T(8,128)(2,1)S(1)}, u32[]{:S(2)}, u32[]{:S(2)}) collective-permute-start(bf16[2,64,1280]{2,1,0:T(8,128)(2,1)S(1)} %pad_maximum_fusion.3.refs_1_), channel_id=1, source_target_pairs={{0,128},{32,160},{64,192},{96,224},{128,0},{160,32},{192,64},{224,... | collective-permute-start | bytes 983048 | tf_op jit(solution)/shard_map/ppermute | solution.py:326
  68.7 10.9 %collective-permute-start.11 = (bf16[2,64,1280]{2,1,0:T(8,128)(2,1)S(1)}, bf16[2,64,1280]{2,1,0:T(8,128)(2,1)S(1)}, u32[]{:S(2)}, u32[]{:S(2)}) collective-permute-start(bf16[2,64,1280]{2,1,0:T(8,128)(2,1)S(1)} %get-tuple-element.102), channel_id=1, source_target_pairs={{0,96},{32,64},{64,32},{96,0},{128,224},{160,192},{192,160},{224,1... | collective-permute-start | bytes 983048 | tf_op jit(solution)/shard_map/ppermute | solution.py:326
  70.0 9.7 %collective-permute-start.12 = (bf16[2,64,1280]{2,1,0:T(8,128)(2,1)S(1)}, bf16[2,64,1280]{2,1,0:T(8,128)(2,1)S(1)}, u32[]{:S(2)}, u32[]{:S(2)}) collective-permute-start(bf16[2,64,1280]{2,1,0:T(8,128)(2,1)S(1)} %get-tuple-element.104), channel_id=1, source_target_pairs={{0,128},{32,160},{64,192},{96,224},{128,0},{160,32},{192,64},{224,... | collective-permute-start | bytes 983048 | tf_op jit(solution)/shard_map/ppermute | solution.py:326
  76.6 14.1 %collective-permute-start.19 = (bf16[2560,128]{1,0:T(8,128)(2,1)S(1)}, bf16[2560,128]{1,0:T(8,128)(2,1)S(1)}, u32[]{:S(2)}, u32[]{:S(2)}) collective-permute-start(bf16[2560,128]{1,0:T(8,128)(2,1)S(1)} %get-tuple-element.125), channel_id=1, source_target_pairs={{0,32},{32,0},{64,96},{96,64},{128,160},{160,128},{192,224},{224,1... | collective-permute-start | bytes 1966088 | tf_op jit(solution)/shard_map/ppermute | solution.py:326
  79.8 5.5 %collective-permute-start.18 = (bf16[64,1280]{1,0:T(8,128)(2,1)S(1)}, bf16[64,1280]{1,0:T(8,128)(2,1)S(1)}, u32[]{:S(2)}, u32[]{:S(2)}) collective-permute-start(bf16[64,1280]{1,0:T(8,128)(2,1)S(1)} %slice_bitcast_fusion), channel_id=1, source_target_pairs={{0,96},{32,64},{64,32},{96,0},{128,224},{160,192},{192,160},{224,1... | collective-permute-start | bytes 491528 | tf_op jit(solution)/shard_map/ppermute | solution.py:326
  81.2 4.6 %collective-permute-start.17 = (bf16[64,1280]{1,0:T(8,128)(2,1)S(1)}, bf16[64,1280]{1,0:T(8,128)(2,1)S(1)}, u32[]{:S(2)}, u32[]{:S(2)}) collective-permute-start(bf16[64,1280]{1,0:T(8,128)(2,1)S(1)} %slice_bitcast_fusion.1), channel_id=1, source_target_pairs={{0,128},{32,160},{64,192},{96,224},{128,0},{160,32},{192,64},{224,... | collective-permute-start | bytes 491528 | tf_op jit(solution)/shard_map/ppermute | solution.py:326
  81.9 7.1 %collective-permute-start.13 = (bf16[2,64,1280]{2,1,0:T(8,128)(2,1)S(1)}, bf16[2,64,1280]{2,1,0:T(8,128)(2,1)S(1)}, u32[]{:S(2)}, u32[]{:S(2)}) collective-permute-start(bf16[2,64,1280]{2,1,0:T(8,128)(2,1)S(1)} %get-tuple-element.112), channel_id=1, source_target_pairs={{0,96},{32,64},{64,32},{96,0},{128,224},{160,192},{192,160},{224,1... | collective-permute-start | bytes 983048 | tf_op jit(solution)/shard_map/ppermute | solution.py:326
  83.0 6.2 %collective-permute-start.14 = (bf16[2,64,1280]{2,1,0:T(8,128)(2,1)S(1)}, bf16[2,64,1280]{2,1,0:T(8,128)(2,1)S(1)}, u32[]{:S(2)}, u32[]{:S(2)}) collective-permute-start(bf16[2,64,1280]{2,1,0:T(8,128)(2,1)S(1)} %get-tuple-element.114), channel_id=1, source_target_pairs={{0,128},{32,160},{64,192},{96,224},{128,0},{160,32},{192,64},{224,... | collective-permute-start | bytes 983048 | tf_op jit(solution)/shard_map/ppermute | solution.py:326
  89.4 6.1 %collective-permute-start.15 = (bf16[64,1280]{1,0:T(8,128)(2,1)S(1)}, bf16[64,1280]{1,0:T(8,128)(2,1)S(1)}, u32[]{:S(2)}, u32[]{:S(2)}) collective-permute-start(bf16[64,1280]{1,0:T(8,128)(2,1)S(1)} %get-tuple-element.151), channel_id=1, source_target_pairs={{0,128},{32,160},{64,192},{96,224},{128,0},{160,32},{192,64},{224,... | collective-permute-start | bytes 491528 | tf_op jit(solution)/shard_map/ppermute | solution.py:326
  90.7 6.2 %collective-permute-start.20 = (bf16[128,1280]{1,0:T(8,128)(2,1)S(1)}, bf16[128,1280]{1,0:T(8,128)(2,1)S(1)}, u32[]{:S(2)}, u32[]{:S(2)}) collective-permute-start(bf16[128,1280]{1,0:T(8,128)(2,1)S(1)} %pad_maximum_fusion.4), channel_id=1, source_target_pairs={{0,32},{32,0},{64,96},{96,64},{128,160},{160,128},{192,224},{224,1... | collective-permute-start | bytes 983048 | tf_op jit(solution)/shard_map/ppermute | solution.py:326
  90.9 6.0 %collective-permute-start.16 = (bf16[64,1280]{1,0:T(8,128)(2,1)S(1)}, bf16[64,1280]{1,0:T(8,128)(2,1)S(1)}, u32[]{:S(2)}, u32[]{:S(2)}) collective-permute-start(bf16[64,1280]{1,0:T(8,128)(2,1)S(1)} %get-tuple-element.149), channel_id=1, source_target_pairs={{0,96},{32,64},{64,32},{96,0},{128,224},{160,192},{192,160},{224,1... | collective-permute-start | bytes 491528 | tf_op jit(solution)/shard_map/ppermute | solution.py:326
  98.2 36.3 %all-to-all-start.1 = ((bf16[32,8,1280]{2,1,0:T(8,128)(2,1)}), bf16[32,8,1280]{2,1,0:T(8,128)(2,1)S(1)}, u32[]{:S(2)}, u32[]{:S(2)}) async-start(bf16[32,8,1280]{2,1,0:T(8,128)(2,1)} %bitcast.16), calls=%async_computation.1 | async-start | bytes 1310720 | tf_op jit(solution)/shard_map/all_to_all | solution.py:293
  114.7 55.0 %collective-permute-start.22 = (bf16[5120,128]{1,0:T(8,128)(2,1)}, bf16[5120,128]{1,0:T(8,128)(2,1)S(1)}, u32[]{:S(2)}, u32[]{:S(2)}) collective-permute-start(bf16[5120,128]{1,0:T(8,128)(2,1)} %copy-done.10), channel_id=1, source_target_pairs={{0,32},{32,0},{64,96},{96,64},{128,160},{160,128},{192,224},{224,1... | collective-permute-start | bytes 3932168 | tf_op jit(solution)/shard_map/ppermute | solution.py:326
  137.9 2.2 %collective-permute-start.21 = (bf16[640,128]{1,0:T(8,128)(2,1)S(1)}, bf16[640,128]{1,0:T(8,128)(2,1)S(1)}, u32[]{:S(2)}, u32[]{:S(2)}) collective-permute-start(bf16[640,128]{1,0:T(8,128)(2,1)S(1)} %get-tuple-element.134), channel_id=1, source_target_pairs={{0,1},{1,0},{2,3},{3,2},{4,5},{5,4},{6,7},{7,6},{8,9},{9,8},{10,11... | collective-permute-start | bytes 491528 | tf_op jit(solution)/shard_map/ppermute | solution.py:301
  163.0 11.3 %all-to-all-start.4 = ((bf16[16,40,128]{2,1,0:T(8,128)(2,1)}), bf16[16,40,128]{2,1,0:T(8,128)(2,1)S(1)}, u32[]{:S(2)}, u32[]{:S(2)}) async-start(bf16[16,40,128]{2,1,0:T(8,128)(2,1)} %share_z.1), calls=%async_computation.4 | async-start | bytes 327680 | tf_op jit(solution)/shard_map/all_to_all | solution.py:293
  174.3 5.4 %collective-permute-start.23 = (bf16[16,40,128]{2,1,0:T(8,128)(2,1)S(1)}, bf16[16,40,128]{2,1,0:T(8,128)(2,1)S(1)}, u32[]{:S(2)}, u32[]{:S(2)}) collective-permute-start(bf16[16,40,128]{2,1,0:T(8,128)(2,1)S(1)} %all-to-all-done.4.kept), channel_id=1, source_target_pairs={{0,1},{1,0},{2,3},{3,2},{4,5},{5,4},{6,7},{7,6},{8,9},{9,8},{10,11... | collective-permute-start | bytes 491528 | tf_op jit(solution)/shard_map/ppermute | solution.py:308
  (5 other events, 5.8 us)
